TPU v7x, 256 devices: a whole 4x4x8 slice. The times are simulated.
256 devices in a mesh: dp: 4 (over x), ctx: 16 (over z, core), exp: 4 (over y).
Axes of the slice: x: 4, y: 4, z: 8, core: 2. Of those that a mesh axis runs over, the one named last changes fastest.
Arguments:
- queries: bfloat16 [4, 8192, 1024], P('dp', 'ctx', 'exp'), may hold values from -6 to 6
- key_rows: bfloat16 [4, 8192, 1024], P('dp', 'ctx', 'exp'), may hold values from -6 to 6
- value_rows: bfloat16 [4, 8192, 1024], P('dp', 'ctx', 'exp'), may hold values from -6 to 6
- segments: int32 [4, 8192], P('dp', 'ctx'), may hold values from 0 to 7, never falling along the last dimension, each value on 1 to 2048 neighbouring positions
- left_blocks: int32 [4, 128, 3], P('dp', 'ctx'), may hold values from -1 to 126, as said below
- moe_input: bfloat16 [4, 8192, 1024], P('dp', ('ctx', 'exp')), may hold values from -6 to 6
- out_grad: bfloat16 [4, 8192, 1024], P('dp', ('ctx', 'exp')), may hold values from -6 to 6
- expert_ids: int32 [4, 8192, 2], P('dp', ('ctx', 'exp')), may hold values from 0 to 63, all different within a row; in each aligned block of 128 rows (0 to 127, 128 to 255, ..., all dimensions but the last counted through in order) at most 8 rows name the same one
- gate_weights: bfloat16 [4, 8192, 2], P('dp', ('ctx', 'exp')), may hold values from 0.19921875 to 1
- expert_in: bfloat16 [64, 1024, 1024], P(('ctx', 'exp')), may hold values from -0.1875 to 0.1875
- expert_out: bfloat16 [64, 1024, 1024], P(('ctx', 'exp')), may hold values from -0.1875 to 0.1875
Outputs:
- d_queries: bfloat16 [4, 8192, 1024], P('dp', 'ctx', 'exp')
- d_keys: bfloat16 [4, 8192, 1024], P('dp', 'ctx', 'exp')
- d_values: bfloat16 [4, 8192, 1024], P('dp', 'ctx', 'exp')
- d_residual: bfloat16 [4, 8192, 1024], P('dp', ('ctx', 'exp'))
- d_gates: bfloat16 [4, 8192, 2], P('dp', ('ctx', 'exp'))
- d_expert_in: bfloat16 [64, 1024, 1024], P(('ctx', 'exp'))
- d_expert_out: bfloat16 [64, 1024, 1024], P(('ctx', 'exp'))
Inputs may be any that keep to these rules, and one draw needn't show every extreme that they name: `left_blocks`: entries of group c (counted from 0 in its batch) are -1 or distinct groups from c - 8 to c - 1; every odd group c of 8 or more lists group c - 8. `expert_ids`: in the 128 rows of one device no expert is named by more than 8 rows, and in some aligned block one expert is named by exactly 8.
All inputs are finite; a program needn't handle non-finite values.
Results may differ from a plain program's by a relative error of at most 0.013.
Values may be sent and summed in bfloat16 or wider, within the bound.
A program may use at most 128 MiB of HBM per device.

v0:
```python
import jax
import jax.numpy as jnp
from jax import lax
from jax.sharding import PartitionSpec as P

DH = 64
CH = 64


masked_score = -1e30


def from_behind(block, axis, distance):
    devices = range(lax.axis_size(axis))
    route = [(i - distance, i) for i in devices if i - distance in devices]
    return lax.ppermute(block, axis, route)


def expert_backward(inputs):
    weight_in, weight_out, rows_in, rows_grad, gate_rows = inputs
    pre = jnp.dot(rows_in, weight_in, preferred_element_type=jnp.float32)
    sigma = jax.nn.sigmoid(pre)
    active = (pre * sigma).astype(jnp.bfloat16)
    produced = jnp.dot(active, weight_out, preferred_element_type=jnp.float32)
    gate_grad = jnp.sum(produced * rows_grad.astype(jnp.float32), axis=1).astype(jnp.bfloat16)
    scaled = (gate_rows.astype(jnp.float32)[:, None] * rows_grad.astype(jnp.float32)).astype(
        jnp.bfloat16
    )
    grad_out = lax.dot_general(
        active, scaled, (((0,), (0,)), ((), ())), preferred_element_type=jnp.float32
    )
    grad_active = lax.dot_general(
        scaled, weight_out, (((1,), (1,)), ((), ())), preferred_element_type=jnp.float32
    )
    grad_pre = (grad_active * sigma * (1.0 + pre * (1.0 - sigma))).astype(jnp.bfloat16)
    grad_in = lax.dot_general(
        rows_in, grad_pre, (((0,), (0,)), ((), ())), preferred_element_type=jnp.float32
    )
    back = lax.dot_general(
        grad_pre, weight_in, (((1,), (1,)), ((), ())), preferred_element_type=jnp.float32
    ).astype(jnp.bfloat16)
    return (grad_in, grad_out, back, gate_grad)


def attention_grads(queries, key_rows, value_rows, grad_rows, segments, blocks):
    frames, local_width = queries.shape
    n_groups = frames // CH
    heads = local_width // DH
    listed = blocks.shape[1] + 1
    score_scale = DH ** (-0.5)
    shard = lax.axis_index("ctx")
    seg_half = segments.astype(jnp.bfloat16)
    prior = from_behind((key_rows, value_rows, seg_half), "ctx", 1)
    key_all = jnp.concatenate([prior[0], key_rows], axis=0).reshape(2 * n_groups, CH, heads, DH)
    value_all = jnp.concatenate([prior[1], value_rows], axis=0).reshape(2 * n_groups, CH, heads, DH)
    seg_all = jnp.concatenate([prior[2], seg_half], axis=0).reshape(2 * n_groups, CH)
    group_ids = shard * n_groups + jnp.arange(n_groups, dtype=jnp.int32)
    lists = jnp.concatenate([group_ids[:, None], blocks], axis=1)
    present = lists >= 0
    local_index = jnp.where(present, lists - (shard - 1) * n_groups, 0)
    key_blocks = key_all[local_index].reshape(n_groups, listed * CH, heads, DH)
    value_blocks = value_all[local_index].reshape(n_groups, listed * CH, heads, DH)
    seg_keys = seg_all[local_index].reshape(n_groups, listed * CH)
    seg_query = seg_half.reshape(n_groups, CH)
    allowed = jnp.repeat(present, CH, axis=1)[:, None, :] & (
        seg_query[:, :, None] == seg_keys[:, None, :]
    )
    query_c = queries.reshape(n_groups, CH, heads, DH)
    grad_c = grad_rows.reshape(n_groups, CH, heads, DH)
    scores = (
        jnp.einsum("cqhd,ckhd->chqk", query_c, key_blocks, preferred_element_type=jnp.float32)
        * score_scale
    )
    scores = jnp.where(allowed[:, None], scores, masked_score)
    row_max = jnp.max(scores, axis=3, keepdims=True)
    log_total = row_max + jnp.log(jnp.sum(jnp.exp(scores - row_max), axis=3, keepdims=True))
    weights = jnp.exp(scores - log_total)
    probs = weights.astype(jnp.bfloat16)
    attended = jnp.einsum(
        "chqk,ckhd->cqhd", probs, value_blocks, preferred_element_type=jnp.float32
    )
    delta = jnp.transpose(jnp.sum(grad_c.astype(jnp.float32) * attended, axis=3), (0, 2, 1))[
        ..., None
    ]
    grad_probs = jnp.einsum(
        "cqhd,ckhd->chqk", grad_c, value_blocks, preferred_element_type=jnp.float32
    )
    dscore = (weights * (grad_probs - delta)).astype(jnp.bfloat16)
    grad_query = (
        jnp.einsum("chqk,ckhd->cqhd", dscore, key_blocks, preferred_element_type=jnp.float32)
        * score_scale
    )
    key_terms = (
        jnp.einsum("chqk,cqhd->ckhd", dscore, query_c, preferred_element_type=jnp.float32)
        * score_scale
    )
    value_terms = jnp.einsum("chqk,cqhd->ckhd", probs, grad_c, preferred_element_type=jnp.float32)
    selector = (
        (local_index[:, :, None] == jnp.arange(2 * n_groups, dtype=jnp.int32)) & present[:, :, None]
    ).astype(jnp.float32)
    key_sum = jnp.einsum(
        "cwm,cwx->mx",
        selector,
        key_terms.reshape(n_groups, listed, CH * local_width),
        precision=lax.Precision.HIGHEST,
    )
    value_sum = jnp.einsum(
        "cwm,cwx->mx",
        selector,
        value_terms.reshape(n_groups, listed, CH * local_width),
        precision=lax.Precision.HIGHEST,
    )
    returned = (
        from_behind(key_sum[:n_groups].astype(jnp.bfloat16), "ctx", -1).astype(jnp.float32),
        from_behind(value_sum[:n_groups].astype(jnp.bfloat16), "ctx", -1).astype(jnp.float32),
    )
    grad_keys = (key_sum[n_groups:] + returned[0]).reshape(frames, local_width).astype(jnp.bfloat16)
    grad_values = (
        (value_sum[n_groups:] + returned[1]).reshape(frames, local_width).astype(jnp.bfloat16)
    )
    return (grad_query.reshape(frames, local_width).astype(jnp.bfloat16), grad_keys, grad_values)


def local(
    queries,
    key_rows,
    value_rows,
    segments,
    left_blocks,
    moe_input,
    out_grad,
    expert_ids,
    gate_weights,
    expert_in,
    expert_out,
):
    n_ctx = lax.axis_size("ctx")
    n_exp = lax.axis_size("exp")
    experts = n_ctx * n_exp
    tokens = moe_input.shape[1]
    width = moe_input.shape[2]
    capacity = 4 * tokens // experts
    routes = expert_ids[0].reshape(-1)
    onehot = (routes[:, None] == jnp.arange(experts, dtype=jnp.int32)).astype(jnp.int32)
    earlier = jnp.cumsum(onehot, axis=0) - onehot
    position = routes * capacity + jnp.sum(earlier * onehot, axis=1)
    source = (
        jnp.full((experts * capacity,), -1, jnp.int32)
        .at[position]
        .set(jnp.arange(2 * tokens, dtype=jnp.int32))
    )
    filled = source >= 0
    chosen = jnp.where(filled, source, 0)
    zero_half = jnp.zeros((), jnp.bfloat16)
    rows_in = jnp.where(filled[:, None], moe_input[0][chosen // 2], zero_half).reshape(
        experts, capacity, width
    )
    rows_grad = jnp.where(filled[:, None], out_grad[0][chosen // 2], zero_half).reshape(
        experts, capacity, width
    )
    gate_rows = jnp.where(filled, gate_weights[0].reshape(-1)[chosen], zero_half).reshape(
        experts, capacity
    )
    arrived = (
        lax.all_to_all(rows_in, ("ctx", "exp"), split_axis=0, concat_axis=0, tiled=True),
        lax.all_to_all(rows_grad, ("ctx", "exp"), split_axis=0, concat_axis=0, tiled=True),
        lax.all_to_all(gate_rows, ("ctx", "exp"), split_axis=0, concat_axis=0, tiled=True),
    )
    grad_in, grad_out, back, gate_grad = expert_backward(
        (
            expert_in[0],
            expert_out[0],
            arrived[0].reshape(-1, width),
            arrived[1].reshape(-1, width),
            arrived[2].reshape(-1),
        )
    )
    returned = (
        lax.all_to_all(
            back.reshape(experts, capacity, width),
            ("ctx", "exp"),
            split_axis=0,
            concat_axis=0,
            tiled=True,
        ),
        lax.all_to_all(
            gate_grad.reshape(experts, capacity),
            ("ctx", "exp"),
            split_axis=0,
            concat_axis=0,
            tiled=True,
        ),
    )
    back_rows = returned[0].reshape(-1, width)[position].reshape(tokens, 2, width)
    d_residual = (
        out_grad[0].astype(jnp.float32) + jnp.sum(back_rows.astype(jnp.float32), axis=1)
    ).astype(jnp.bfloat16)
    d_gates = returned[1].reshape(-1)[position].reshape(tokens, 2)
    summed = (
        lax.psum(grad_in.astype(jnp.bfloat16), "dp").astype(jnp.float32),
        lax.psum(grad_out.astype(jnp.bfloat16), "dp").astype(jnp.float32),
    )
    grad_local = lax.all_to_all(d_residual, "exp", split_axis=1, concat_axis=0, tiled=True)
    grad_query, grad_keys, grad_values = attention_grads(
        queries[0], key_rows[0], value_rows[0], grad_local, segments[0], left_blocks[0]
    )
    return (
        grad_query[None],
        grad_keys[None],
        grad_values[None],
        d_residual[None],
        d_gates[None],
        summed[0].astype(jnp.bfloat16)[None],
        summed[1].astype(jnp.bfloat16)[None],
    )


def solution(mesh):
    return jax.shard_map(
        local,
        mesh=mesh,
        in_specs=(
            P("dp", "ctx", "exp"),
            P("dp", "ctx", "exp"),
            P("dp", "ctx", "exp"),
            P("dp", "ctx"),
            P("dp", "ctx", None),
            P("dp", ("ctx", "exp"), None),
            P("dp", ("ctx", "exp"), None),
            P("dp", ("ctx", "exp"), None),
            P("dp", ("ctx", "exp"), None),
            P(("ctx", "exp"), None, None),
            P(("ctx", "exp"), None, None),
        ),
        out_specs=(
            P("dp", "ctx", "exp"),
            P("dp", "ctx", "exp"),
            P("dp", "ctx", "exp"),
            P("dp", ("ctx", "exp"), None),
            P("dp", ("ctx", "exp"), None),
            P(("ctx", "exp"), None, None),
            P(("ctx", "exp"), None, None),
        ),
        check_vma=False,
    )
```

profile of v0, /device:TPU:1, one launch (start us, length us, event | category | flops | bytes accessed | tf_op | source)
XLA Modules:
  0.0 304.9 jit_solution(6219015213937808891)
XLA Ops:
  12.7 3.4 %gather_fusion.2 = bf16[512]{0:T(512)(128)(2,1)S(1)} fusion(bf16[256]{0:T(256)(128)(2,1)S(1)} %reshape_squeeze.8, s32[1024]{0:T(1024)S(1)} %pad_clamp_fusion.2), kind=kCustom, calls=%fused_computation.2 | custom fusion | bytes 4096 | tf_op jit(solution)/shard_map/gather | solution.py:161
  16.8 13.2 %all-to-all-start = ((bf16[64,1,8]{2,1,0:T(2,128)(2,1)}), bf16[64,1,8]{2,1,0:T(2,128)(2,1)S(1)}, u32[]{:S(2)}, u32[]{:S(2)}) async-start(bf16[64,1,8]{2,1,0:T(2,128)(2,1)} %all_to_all.37), calls=%async_computation | async-start | bytes 65536 | tf_op jit(solution)/shard_map/all_to_all | solution.py:167
  30.1 2.8 gather_fusion.4
  32.9 2.8 gather_fusion.3
  35.7 2.8 bitcast_select_fusion.2
  39.1 37.7 %all_to_all.44 = bf16[64,8,1024]{2,1,0:T(8,128)(2,1)} all-to-all(bf16[64,8,1024]{2,1,0:T(8,128)(2,1)} %get-tuple-element.40), channel_id=1, replica_groups=mesh['dp'=4,'ctx'=16,'exp'=4] {'ctx','exp'}, dimensions={0} | all-to-all | bytes 2097152 | tf_op jit(solution)/shard_map/all_to_all | solution.py:165
  76.8 6.7 %all-to-all-start.1 = ((bf16[64,8,1024]{2,1,0:T(8,128)(2,1)}), bf16[64,8,1024]{2,1,0:T(8,128)(2,1)}, u32[]{:S(2)}, u32[]{:S(2)}) async-start(bf16[64,8,1024]{2,1,0:T(8,128)(2,1)} %get-tuple-element.39), calls=%async_computation.1 | async-start | bytes 2097152 | tf_op jit(solution)/shard_map/all_to_all | solution.py:166
  83.5 3.5 %collective-permute-start.1 = (bf16[512]{0:T(512)(128)(2,1)S(1)}, bf16[512]{0:T(512)(128)(2,1)S(1)}, u32[]{:S(2)}, u32[]{:S(2)}) collective-permute-start(bf16[512]{0:T(512)(128)(2,1)S(1)} %convert_reduce_fusion), channel_id=1, source_target_pairs={{0,4},{4,8},{8,12},{12,16},{16,20},{20,24},{24,28},{28,32},{32,36}... | collective-permute-start | bytes 3080 | tf_op jit(solution)/shard_map/ppermute | solution.py:16
  89.1 3.3 %collective-permute-start.2 = (bf16[512,256]{1,0:T(8,128)(2,1)S(1)}, bf16[512,256]{1,0:T(8,128)(2,1)}, u32[]{:S(2)}, u32[]{:S(2)}) collective-permute-start(bf16[512,256]{1,0:T(8,128)(2,1)S(1)} %bitcast.133), channel_id=1, source_target_pairs={{0,4},{4,8},{8,12},{12,16},{16,20},{20,24},{24,28},{28,32},{32,36}... | collective-permute-start | bytes 786440 | tf_op jit(solution)/shard_map/ppermute | solution.py:16
  96.0 6.5 %collective-permute-done.1 = bf16[512]{0:T(512)(128)(2,1)S(1)} collective-permute-done((bf16[512]{0:T(512)(128)(2,1)S(1)}, bf16[512]{0:T(512)(128)(2,1)S(1)}, u32[]{:S(2)}, u32[]{:S(2)}) %collective-permute-start.1) | collective-permute-done | bytes 1056 | tf_op jit(solution)/shard_map/ppermute | solution.py:16
  103.3 3.8 %fusion.7 = f32[512,1024]{1,0:T(8,128)} fusion(bf16[1,1024,1024]{2,1,0:T(8,128)(2,1)S(1)} %copy-done, bf16[64,8,1024]{2,1,0:T(8,128)(2,1)} %all_to_all.44), kind=kOutput, calls=%fused_computation.20 | convolution fusion | flops 1073741824 | bytes 5242880 | tf_op jit(solution)/shard_map/dot_general | solution.py:21
  107.2 4.0 %all-to-all-done.1 = bf16[64,8,1024]{2,1,0:T(8,128)(2,1)} async-done(((bf16[64,8,1024]{2,1,0:T(8,128)(2,1)}), bf16[64,8,1024]{2,1,0:T(8,128)(2,1)}, u32[]{:S(2)}, u32[]{:S(2)}) %all-to-all-start.1) | async-done | bytes 1048608 | tf_op jit(solution)/shard_map/all_to_all | solution.py:166
  111.1 3.8 %fusion.2 = bf16[512]{0:T(512)(128)(2,1)S(1)} fusion(bf16[64,8,1024]{2,1,0:T(8,128)(2,1)} %all-to-all-done.1, bf16[1,1024,1024]{2,1,0:T(8,128)(2,1)} %param.21, f32[512,1024]{1,0:T(8,128)} %fusion.7), kind=kOutput, calls=%fused_computation.15 | convolution fusion | flops 1077935616 | bytes 5243904 | tf_op jit(solution)/shard_map/dot_general | solution.py:24
  115.7 21.5 %all-to-all-start.5 = ((bf16[64,1,8]{2,1,0:T(2,128)(2,1)}), bf16[64,1,8]{2,1,0:T(2,128)(2,1)S(1)}, u32[]{:S(2)}, u32[]{:S(2)}) async-start(bf16[64,1,8]{2,1,0:T(2,128)(2,1)} %convert_element_type.217), calls=%async_computation.5 | async-start | bytes 65536 | tf_op jit(solution)/shard_map/all_to_all | solution.py:186
  137.2 4.2 %multiply_convert_fusion.2 = bf16[512,1024]{1,0:T(8,128)(2,1)S(1)} fusion(f32[512,1024]{1,0:T(8,128)} %fusion.7, bf16[1,1024,1024]{2,1,0:T(8,128)(2,1)} %param.21, bf16[64,8,1024]{2,1,0:T(8,128)(2,1)} %all-to-all-done.1, f32[64,8]{1,0:T(8,128)S(1)} %bitcast.140), kind=kOutput, calls=%fused_computation.34 | convolution fusion | flops 1080033280 | bytes 6293504 | tf_op jit(solution)/shard_map/dot_general | solution.py:32
  146.2 9.0 %all-to-all-start.3 = ((bf16[64,8,1024]{2,1,0:T(8,128)(2,1)}), bf16[64,8,1024]{2,1,0:T(8,128)(2,1)S(1)}, u32[]{:S(2)}, u32[]{:S(2)}) async-start(bf16[64,8,1024]{2,1,0:T(8,128)(2,1)} %fusion.21), calls=%async_computation.3 | async-start | bytes 2097152 | tf_op jit(solution)/shard_map/all_to_all | solution.py:179
  163.4 5.3 %copy.110 = bf16[32,64,4,64]{1,0,3,2:T(8,128)(2,1)} copy(bf16[32,64,4,64]{3,1,2,0:T(8,128)(2,1)} %gather_fusion) | data formatting | bytes 2097152 | tf_op jit(solution)/shard_map/gather | solution.py:61
  168.7 4.1 %reshape.315 = bf16[8,256,4,64]{1,0,3,2:T(8,128)(2,1)} reshape(bf16[32,64,4,64]{1,0,3,2:T(8,128)(2,1)} %copy.110) | data formatting | bytes 2097152 | tf_op jit(solution)/shard_map/reshape | solution.py:61
  174.9 5.3 %copy.125 = bf16[32,64,4,64]{1,0,3,2:T(8,128)(2,1)} copy(bf16[32,64,4,64]{3,1,2,0:T(8,128)(2,1)} %gather_fusion.6) | data formatting | bytes 2097152 | tf_op jit(solution)/shard_map/gather | solution.py:62
  180.2 4.2 %reshape.322 = bf16[8,256,4,64]{1,0,3,2:T(8,128)(2,1)} reshape(bf16[32,64,4,64]{1,0,3,2:T(8,128)(2,1)} %copy.125) | data formatting | bytes 2097152 | tf_op jit(solution)/shard_map/reshape | solution.py:62
  187.3 2.6 convert_bitcast_fusion.2
  189.9 4.0 %convert_bitcast_fusion.1 = bf16[1,1024,1024]{2,1,0:T(8,128)(2,1)} fusion(bf16[64,8,1024]{2,1,0:T(8,128)(2,1)} %all-to-all-done.1, f32[512]{0:T(512)S(1)} %reshape.330, f32[512,1024]{1,0:T(8,128)S(1)} %copy-done.28), kind=kOutput, calls=%fused_computation.29 | convolution fusion | flops 1078984704 | bytes 5244928 | tf_op jit(solution)/shard_map/dot_general | solution.py:29
  203.8 4.2 %all-to-all-start.4 = ((bf16[128,4,256]{0,2,1:T(8,128)(2,1)}), bf16[128,4,256]{0,2,1:T(8,128)(2,1)}, u32[]{:S(2)}, u32[]{:S(2)}) async-start(bf16[128,4,256]{0,2,1:T(8,128)(2,1)} %add_convert_fusion), calls=%async_computation.4 | async-start | bytes 524288 | tf_op jit(solution)/shard_map/all_to_all | solution.py:203
  208.8 5.1 %all-to-all-done.4 = bf16[128,4,256]{0,2,1:T(8,128)(2,1)} async-done(((bf16[128,4,256]{0,2,1:T(8,128)(2,1)}), bf16[128,4,256]{0,2,1:T(8,128)(2,1)}, u32[]{:S(2)}, u32[]{:S(2)}) %all-to-all-start.4) | async-done | bytes 262176 | tf_op jit(solution)/shard_map/all_to_all | solution.py:203
  220.7 3.2 %copy.133 = f32[8,256,4,64]{3,2,1,0:T(4,128)} copy(f32[8,256,4,64]{1,3,2,0:T(8,128)S(1)} %multiply_bitcast_fusion) | data formatting | bytes 4194304 | tf_op jit(solution)/shard_map/mul | solution.py:94
  223.9 4.7 %reshape.323 = f32[8,4,16384]{2,1,0:T(4,128)S(1)} reshape(f32[8,256,4,64]{3,2,1,0:T(4,128)} %copy.133) | data formatting | bytes 4194304 | tf_op jit(solution)/shard_map/reshape | solution.py:104
  230.6 3.8 %collective-permute-start.3 = (bf16[8,16384]{1,0:T(8,128)(2,1)S(1)}, bf16[8,16384]{1,0:T(8,128)(2,1)}, u32[]{:S(2)}, u32[]{:S(2)}) collective-permute-start(bf16[8,16384]{1,0:T(8,128)(2,1)S(1)} %slice.57), channel_id=1, source_target_pairs={{4,0},{8,4},{12,8},{16,12},{20,16},{24,20},{28,24},{32,28},{36,32}... | collective-permute-start | bytes 786440 | tf_op jit(solution)/shard_map/ppermute | solution.py:16
  240.0 3.4 %copy.136 = f32[8,256,4,64]{3,2,1,0:T(4,128)} copy(f32[8,256,4,64]{1,3,2,0:T(8,128)S(1)} %copy-done.6) | data formatting | bytes 4194304 | tf_op jit(solution)/shard_map/chqk,cqhd->ckhd/transpose | solution.py:97
  243.4 4.6 %reshape.324 = f32[8,4,16384]{2,1,0:T(4,128)S(1)} reshape(f32[8,256,4,64]{3,2,1,0:T(4,128)} %copy.136) | data formatting | bytes 4194304 | tf_op jit(solution)/shard_map/reshape | solution.py:110
  254.8 4.3 %collective-permute-done.4 = bf16[8,16384]{1,0:T(8,128)(2,1)S(1)} collective-permute-done((bf16[8,16384]{1,0:T(8,128)(2,1)S(1)}, bf16[8,16384]{1,0:T(8,128)(2,1)S(1)}, u32[]{:S(2)}, u32[]{:S(2)}) %collective-permute-start.4) | collective-permute-done | bytes 262176 | tf_op jit(solution)/shard_map/ppermute | solution.py:16
  261.0 32.1 %all-reduce.3.cloned.1.call-done = (bf16[1,1024,1024]{2,1,0:T(8,128)(2,1)}, bf16[1,1024,1024]{2,1,0:T(8,128)(2,1)}) async-done(((bf16[1,1024,1024]{2,1,0:T(8,128)(2,1)}, bf16[1,1024,1024]{2,1,0:T(8,128)(2,1)}), (bf16[1,1024,1024]{2,1,0:T(8,128)(2,1)}, bf16[1,1024,1024]{2,1,0:T(8,128)(2,1)})) %all-reduce.3.cloned.1.call-update) | async-done | bytes 4194320 | tf_op jit(solution)/shard_map/psum | solution.py:200
  293.1 3.2 %copy.173 = bf16[1,1024,1024]{2,1,0:T(8,128)(2,1)} copy(bf16[1,1024,1024]{2,1,0:T(8,128)(2,1)} %get-tuple-element.48) | data formatting | bytes 4194304
  (164 shorter events, 66.7 us)
Async XLA Ops:
  7.2 96.2 %copy-start = (bf16[1,1024,1024]{2,1,0:T(8,128)(2,1)S(1)}, bf16[1,1024,1024]{2,1,0:T(8,128)(2,1)}, u32[]{:S(2)}) copy-start(bf16[1,1024,1024]{2,1,0:T(8,128)(2,1)} %param.20) | copy-start | bytes 6291460
  7.2 22.9 %copy-start.3 = (bf16[1,128,1024]{2,1,0:T(8,128)(2,1)S(1)}, bf16[1,128,1024]{2,1,0:T(8,128)(2,1)}, u32[]{:S(2)}) copy-start(bf16[1,128,1024]{2,1,0:T(8,128)(2,1)} %param.16) | copy-start | bytes 786436
  16.8 22.2 %all-to-all-start = ((bf16[64,1,8]{2,1,0:T(2,128)(2,1)}), bf16[64,1,8]{2,1,0:T(2,128)(2,1)S(1)}, u32[]{:S(2)}, u32[]{:S(2)}) async-start(bf16[64,1,8]{2,1,0:T(2,128)(2,1)} %all_to_all.37), calls=%async_computation | async-start | bytes 65536 | tf_op jit(solution)/shard_map/all_to_all | solution.py:167
  39.1 64.2 %copy-start.17 = (bf16[64,1,8]{2,1,0:T(2,128)(2,1)}, bf16[64,1,8]{2,1,0:T(2,128)(2,1)S(1)}, u32[]{:S(2)}) copy-start(bf16[64,1,8]{2,1,0:T(2,128)(2,1)S(1)} %all-to-all-done) | copy-start | bytes 3076
  39.1 44.4 %copy-start.27 = (s32[1,512]{1,0:T(1,128)S(1)}, s32[1,512]{1,0:T(1,128)}, u32[]{:S(2)}) copy-start(s32[1,512]{1,0:T(1,128)} %param.14) | copy-start | bytes 6148
  39.1 50.0 %copy-start.20 = (bf16[1,512,256]{2,1,0:T(8,128)(2,1)S(1)}, bf16[1,512,256]{2,1,0:T(8,128)(2,1)}, u32[]{:S(2)}) copy-start(bf16[1,512,256]{2,1,0:T(8,128)(2,1)} %param.13) | copy-start | bytes 786436
  39.1 53.4 %copy-start.24 = (s32[1,8,3]{1,0,2:T(1,128)S(1)}, s32[1,8,3]{1,0,2:T(1,128)}, u32[]{:S(2)}) copy-start(s32[1,8,3]{1,0,2:T(1,128)} %param.15) | copy-start | bytes 292
  39.1 55.6 %copy-start.19 = (bf16[1,512,256]{2,1,0:T(8,128)(2,1)S(1)}, bf16[1,512,256]{2,1,0:T(8,128)(2,1)}, u32[]{:S(2)}) copy-start(bf16[1,512,256]{2,1,0:T(8,128)(2,1)} %param.11) | copy-start | bytes 786436
  76.8 34.3 %all-to-all-start.1 = ((bf16[64,8,1024]{2,1,0:T(8,128)(2,1)}), bf16[64,8,1024]{2,1,0:T(8,128)(2,1)}, u32[]{:S(2)}, u32[]{:S(2)}) async-start(bf16[64,8,1024]{2,1,0:T(8,128)(2,1)} %get-tuple-element.39), calls=%async_computation.1 | async-start | bytes 2097152 | tf_op jit(solution)/shard_map/all_to_all | solution.py:166
  83.5 19.0 %collective-permute-start.1 = (bf16[512]{0:T(512)(128)(2,1)S(1)}, bf16[512]{0:T(512)(128)(2,1)S(1)}, u32[]{:S(2)}, u32[]{:S(2)}) collective-permute-start(bf16[512]{0:T(512)(128)(2,1)S(1)} %convert_reduce_fusion), channel_id=1, source_target_pairs={{0,4},{4,8},{8,12},{12,16},{16,20},{20,24},{24,28},{28,32},{32,36}... | collective-permute-start | bytes 3080 | tf_op jit(solution)/shard_map/ppermute | solution.py:16
  87.0 70.3 %collective-permute-start = (bf16[512,256]{1,0:T(8,128)(2,1)}, bf16[512,256]{1,0:T(8,128)(2,1)}, u32[]{:S(2)}, u32[]{:S(2)}) collective-permute-start(bf16[512,256]{1,0:T(8,128)(2,1)} %bitcast), channel_id=1, source_target_pairs={{0,4},{4,8},{8,12},{12,16},{16,20},{20,24},{24,28},{28,32},{32,36}... | collective-permute-start | bytes 786440 | tf_op jit(solution)/shard_map/ppermute | solution.py:16
  89.1 66.5 %collective-permute-start.2 = (bf16[512,256]{1,0:T(8,128)(2,1)S(1)}, bf16[512,256]{1,0:T(8,128)(2,1)}, u32[]{:S(2)}, u32[]{:S(2)}) collective-permute-start(bf16[512,256]{1,0:T(8,128)(2,1)S(1)} %bitcast.133), channel_id=1, source_target_pairs={{0,4},{4,8},{8,12},{12,16},{16,20},{20,24},{24,28},{28,32},{32,36}... | collective-permute-start | bytes 786440 | tf_op jit(solution)/shard_map/ppermute | solution.py:16
  92.8 9.8 %copy-start.25 = (pred[8,4]{0,1:T(4,128)(4,1)}, pred[8,4]{0,1:T(4,128)(4,1)S(1)}, u32[]{:S(2)}) copy-start(pred[8,4]{0,1:T(4,128)(4,1)S(1)} %fusion.61) | copy-start | bytes 100
  115.7 30.5 %all-to-all-start.5 = ((bf16[64,1,8]{2,1,0:T(2,128)(2,1)}), bf16[64,1,8]{2,1,0:T(2,128)(2,1)S(1)}, u32[]{:S(2)}, u32[]{:S(2)}) async-start(bf16[64,1,8]{2,1,0:T(2,128)(2,1)} %convert_element_type.217), calls=%async_computation.5 | async-start | bytes 65536 | tf_op jit(solution)/shard_map/all_to_all | solution.py:186
  144.7 10.5 %copy-start.23 = (pred[8,256]{1,0:T(8,128)(4,1)S(1)}, pred[8,256]{1,0:T(8,128)(4,1)}, u32[]{:S(2)}) copy-start(pred[8,256]{1,0:T(8,128)(4,1)} %and.29) | copy-start | bytes 6148
  144.7 10.7 %copy-start.18 = (bf16[64,1,8]{2,1,0:T(2,128)(2,1)S(1)}, bf16[64,1,8]{2,1,0:T(2,128)(2,1)}, u32[]{:S(2)}) copy-start(bf16[64,1,8]{2,1,0:T(2,128)(2,1)} %copy-done.17) | copy-start | bytes 3076
  146.2 9.4 %copy-start.21 = (bf16[64,1,8]{2,1,0:T(2,128)(2,1)}, bf16[64,1,8]{2,1,0:T(2,128)(2,1)S(1)}, u32[]{:S(2)}) copy-start(bf16[64,1,8]{2,1,0:T(2,128)(2,1)S(1)} %all-to-all-done.5) | copy-start | bytes 3076
  146.2 51.4 %all-to-all-start.3 = ((bf16[64,8,1024]{2,1,0:T(8,128)(2,1)}), bf16[64,8,1024]{2,1,0:T(8,128)(2,1)S(1)}, u32[]{:S(2)}, u32[]{:S(2)}) async-start(bf16[64,8,1024]{2,1,0:T(8,128)(2,1)} %fusion.21), calls=%async_computation.3 | async-start | bytes 2097152 | tf_op jit(solution)/shard_map/all_to_all | solution.py:179
  155.2 137.9 %all-reduce.3.cloned.1.call-start = ((), (), s32[]{:S(2)}) async-start(), calls=%async_computation.6 | async-start | bytes 8388608 | tf_op jit(solution)/shard_map/psum | solution.py:200
  180.2 4.2 %copy-start.7 = (bf16[8,64,4,64]{1,3,2,0:T(8,128)(2,1)S(1)}, bf16[8,64,4,64]{1,3,2,0:T(8,128)(2,1)}, u32[]{:S(2)}) copy-start(bf16[8,64,4,64]{1,3,2,0:T(8,128)(2,1)} %copy.132) | copy-start | bytes 786436
  180.2 4.2 %copy-start.8 = (bf16[8,256,4,64]{1,0,3,2:T(8,128)(2,1)S(1)}, bf16[8,256,4,64]{1,0,3,2:T(8,128)(2,1)}, u32[]{:S(2)}) copy-start(bf16[8,256,4,64]{1,0,3,2:T(8,128)(2,1)} %reshape.315) | copy-start | bytes 3145732
  184.4 2.8 copy-start.30
  201.7 13.6 %copy-start.5 = (f32[8,4,64,256]{3,2,1,0:T(8,128)S(1)}, f32[8,4,64,256]{3,2,1,0:T(8,128)}, u32[]{:S(2)}) copy-start(f32[8,4,64,256]{3,2,1,0:T(8,128)} %copy-done.4) | copy-start | bytes 6291460
  203.8 10.1 %all-to-all-start.4 = ((bf16[128,4,256]{0,2,1:T(8,128)(2,1)}), bf16[128,4,256]{0,2,1:T(8,128)(2,1)}, u32[]{:S(2)}, u32[]{:S(2)}) async-start(bf16[128,4,256]{0,2,1:T(8,128)(2,1)} %add_convert_fusion), calls=%async_computation.4 | async-start | bytes 524288 | tf_op jit(solution)/shard_map/all_to_all | solution.py:203
  223.9 4.7 %copy-start.26 = (pred[8,4]{0,1:T(4,128)(4,1)S(1)}, pred[8,4]{0,1:T(4,128)(4,1)}, u32[]{:S(2)}) copy-start(pred[8,4]{0,1:T(4,128)(4,1)} %copy-done.25) | copy-start | bytes 100
  228.6 5.8 %copy-start.9 = (bf16[8,256,4,64]{1,0,3,2:T(8,128)(2,1)S(1)}, bf16[8,256,4,64]{1,0,3,2:T(8,128)(2,1)}, u32[]{:S(2)}) copy-start(bf16[8,256,4,64]{1,0,3,2:T(8,128)(2,1)} %reshape.315) | copy-start | bytes 3145732
  228.6 5.8 %copy-start.12 = (bf16[8,4,64,256]{3,2,1,0:T(8,128)(2,1)S(1)}, bf16[8,4,64,256]{3,2,1,0:T(8,128)(2,1)}, u32[]{:S(2)}) copy-start(bf16[8,4,64,256]{3,2,1,0:T(8,128)(2,1)} %copy-done.11) | copy-start | bytes 3145732
  230.6 9.4 %copy-start.6 = (f32[8,256,4,64]{1,3,2,0:T(8,128)S(1)}, f32[8,256,4,64]{1,3,2,0:T(8,128)}, u32[]{:S(2)}) copy-start(f32[8,256,4,64]{1,3,2,0:T(8,128)} %convolution_bitcast_fusion.2) | copy-start | bytes 6291460
  230.6 22.3 %collective-permute-start.3 = (bf16[8,16384]{1,0:T(8,128)(2,1)S(1)}, bf16[8,16384]{1,0:T(8,128)(2,1)}, u32[]{:S(2)}, u32[]{:S(2)}) collective-permute-start(bf16[8,16384]{1,0:T(8,128)(2,1)S(1)} %slice.57), channel_id=1, source_target_pairs={{4,0},{8,4},{12,8},{16,12},{20,16},{24,20},{28,24},{32,28},{36,32}... | collective-permute-start | bytes 786440 | tf_op jit(solution)/shard_map/ppermute | solution.py:16
  251.0 8.1 %collective-permute-start.4 = (bf16[8,16384]{1,0:T(8,128)(2,1)S(1)}, bf16[8,16384]{1,0:T(8,128)(2,1)S(1)}, u32[]{:S(2)}, u32[]{:S(2)}) collective-permute-start(bf16[8,16384]{1,0:T(8,128)(2,1)S(1)} %slice.56), channel_id=1, source_target_pairs={{4,0},{8,4},{12,8},{16,12},{20,16},{24,20},{28,24},{32,28},{36,32}... | collective-permute-start | bytes 786440 | tf_op jit(solution)/shard_map/ppermute | solution.py:16
  293.1 3.2 %copy-start.15 = (bf16[1,1024,1024]{2,1,0:T(8,128)(2,1)S(1)}, bf16[1,1024,1024]{2,1,0:T(8,128)(2,1)}, u32[]{:S(2)}) copy-start(bf16[1,1024,1024]{2,1,0:T(8,128)(2,1)} %get-tuple-element.49) | copy-start | bytes 6291460
  293.1 4.6 %copy-start.1 = (bf16[1,1024,1024]{2,1,0:T(8,128)(2,1)S(1)}, bf16[1,1024,1024]{2,1,0:T(8,128)(2,1)}, u32[]{:S(2)}) copy-start(bf16[1,1024,1024]{2,1,0:T(8,128)(2,1)} %param.20) | copy-start | bytes 6291460
  (10 other events, 18.1 us)
Sparse Core Ops, SparseCore 0:
  194.1 98.9 all-reduce.2
where the time goes:
time: 309 us; the launch traced here: 305 us
  local copies, waits for them, and re-layouts  83.9 us (27%)
  starting transfers between devices  69.2 us (22%)
  waiting for transfers between devices  54.1 us (18%)
  blocking collectives  37.7 us (12%)
  matrix products  31.1 us (10%)
  between operations  15.2 us (5%)
  other arithmetic  13.8 us (4%)
    all_to_all x1, blocking collectives, local(): lax.all_to_all(rows_in, ('ctx', 'exp'), split_axis=0, concat_axis=0, tile...  37.7 us
    psum x1, waiting for transfers between devices, local(): lax.psum(grad_in.astype(jnp.bfloat16), 'dp').astype(jnp.float32)  32.1 us
    all_to_all x1, starting transfers between devices, local(): lax.all_to_all(gate_grad.reshape(experts, capacity), ('ctx', 'exp'), spli...  21.5 us
    unnamed x70, local copies, waits for them, and re-layouts  16.2 us
    ppermute x5, starting transfers between devices, from_behind(): return lax.ppermute(block, axis, route)  14.6 us
    all_to_all x1, starting transfers between devices, local(): lax.all_to_all(gate_rows, ('ctx', 'exp'), split_axis=0, concat_axis=0, ti...  13.2 us
    ppermute x5, waiting for transfers between devices, from_behind(): return lax.ppermute(block, axis, route)  10.8 us
    all_to_all x1, starting transfers between devices, local(): lax.all_to_all(back.reshape(experts, capacity, width), ('ctx', 'exp'), sp...  8.95 us
  transfers between devices with their start and end apart: 11, of which 7 were waited for; matrix products, arithmetic and copies ran while one was open for 36% of the time, Pallas kernels for 0%

commit v1 on v0

v1 whole, which is shorter than its diff:
```python
import functools

import jax
import jax.numpy as jnp
from jax import lax
from jax.experimental import pallas as pl
from jax.experimental.pallas import tpu as pltpu
from jax.sharding import PartitionSpec as P

MESH = pl.DeviceIdType.MESH
BF = jnp.bfloat16
F32 = jnp.float32
I32 = jnp.int32

DP, CTX, EXP = 4, 16, 4
PEERS = CTX * EXP
HALF = CTX // 2
CAP = 8
BLOCK = 2 * CAP
TOKENS = 128
WIDTH = 1024
PART = WIDTH // DP
CHUNKS = 4
PER_CHUNK = PEERS // CHUNKS
CHUNK_ROWS = PER_CHUNK * CAP
GROUP = 64
GROUPS = 8
FRAMES = 512
LOCAL = 256
QROWS = 128
WINDOW = FRAMES + QROWS
FAR = 32768.0
VMEM_BYTES = 50 * 1024 * 1024


def dot(a, b, ca, cb, precision=None):
    return lax.dot_general(
        a, b, (((ca,), (cb,)), ((), ())), preferred_element_type=F32, precision=precision
    )


def wait_bytes(ref, sem):
    pltpu.make_async_copy(ref, ref, sem).wait()


def hop(j):
    s = j // EXP
    return HALF + (2 * (s % 2) - 1) * (s // 2), j % EXP


def moe_kernel(
    x_ref,
    z_ref,
    ids_ref,
    gate_ref,
    win_hbm,
    wout_hbm,
    dres_ref,
    dgate_ref,
    quarter_ref,
    win,
    wout,
    send,
    recv,
    pick_lo,
    pick_hi,
    u_all,
    s_all,
    gp_all,
    act_all,
    bsend,
    brecv,
    hsend,
    hrecv,
    part,
    first,
    second,
    load_sem,
    send_sem,
    recv_sem,
    bsend_sem,
    brecv_sem,
    hsend_sem,
    hrecv_sem,
    dp_send,
    dp_recv,
):
    me_d, me_c, me_x = lax.axis_index("dp"), lax.axis_index("ctx"), lax.axis_index("exp")
    right, left = lax.rem(me_d + 1, DP), lax.rem(me_d + DP - 1, DP)
    load_in = pltpu.make_async_copy(win_hbm, win, load_sem.at[0])
    load_out = pltpu.make_async_copy(wout_hbm, wout, load_sem.at[1])
    load_in.start()
    load_out.start()

    def ahead(k, xo):
        return {"ctx": lax.rem(me_c + k, CTX), "exp": lax.rem(me_x + xo, EXP)}

    def behind(k, xo):
        return {"ctx": lax.rem(me_c - k + CTX, CTX), "exp": lax.rem(me_x - xo + EXP, EXP)}

    barrier = pltpu.get_barrier_semaphore()
    for j in range(1, EXP):
        pl.semaphore_signal(barrier, inc=1, device_id=ahead(0, j), device_id_type=MESH)

    @pl.loop(EXP, PEERS)
    def _(j):
        k, xo = hop(j)
        pl.semaphore_signal(barrier, inc=1, device_id=ahead(k, xo), device_id_type=MESH)

    for other in (left, right):
        pl.semaphore_signal(barrier, inc=1, device_id={"dp": other}, device_id_type=MESH)

    lane64 = lax.broadcasted_iota(I32, (TOKENS, PEERS), 1)
    lane_q = lax.broadcasted_iota(I32, (TOKENS, PEERS * BLOCK), 1)
    ids = ids_ref[...]

    def relative(column):
        k = (column // EXP - me_c + CTX) % CTX
        xo = (column % EXP - me_x + EXP) % EXP
        s = jnp.where(k == 0, 0, jnp.where(k < HALF, CTX - 2 * k, 2 * k - CTX + 1))
        return s * EXP + xo

    peer = [relative(ids[:, t : t + 1]) for t in range(2)]
    named = [(peer[t] == lane64).astype(F32) for t in range(2)]
    before = (
        lax.broadcasted_iota(I32, (TOKENS, TOKENS), 1)
        < lax.broadcasted_iota(I32, (TOKENS, TOKENS), 0)
    ).astype(BF)
    earlier = dot(before, (named[0] + named[1]).astype(BF), 1, 0)
    slot = [
        jnp.sum(named[t] * earlier, axis=1, keepdims=True).astype(I32) for t in range(2)
    ]
    row = [peer[t] * BLOCK + slot[t] for t in range(2)]
    hit_lo = [row[t] == lane_q for t in range(2)]
    hit_hi = [row[t] + CAP == lane_q for t in range(2)]
    pick_lo[...] = (hit_lo[0] | hit_lo[1]).astype(F32).astype(BF)
    pick_hi[...] = (hit_hi[0] | hit_hi[1]).astype(F32).astype(BF)
    gates = gate_ref[...].astype(F32)
    gated = (
        jnp.where(hit_hi[0], gates[:, 0:1], 0.0) + jnp.where(hit_hi[1], gates[:, 1:2], 0.0)
    ).astype(BF)
    second_part = part.at[0, 0]
    second_part[0:TOKENS, :] = gated

    @pl.loop(0, 4)
    def _(t):
        cols = pl.ds(pl.multiple_of(t * 256, 256), 256)
        rows = dot(pick_lo[:, cols], x_ref[...], 0, 0) + dot(
            second_part[0:TOKENS, cols], z_ref[...], 0, 0
        )
        send[pl.ds(t * 16, 16)] = rows.astype(BF).reshape(16, BLOCK, WIDTH)

    pl.semaphore_wait(barrier, PEERS - 1 + 2)

    def dispatch(j, k, xo):
        pltpu.make_async_remote_copy(
            src_ref=send.at[j],
            dst_ref=recv.at[j],
            send_sem=send_sem,
            recv_sem=recv_sem.at[j // EXP],
            device_id=ahead(k, xo),
            device_id_type=MESH,
        ).start()

    @pl.loop(EXP, PEERS)
    def _(j):
        dispatch(j, *hop(j))

    for j in range(1, EXP):
        dispatch(j, 0, j)
    recv[0] = send[0]

    load_in.wait()
    load_out.wait()
    wait_bytes(recv.at[pl.ds(1, EXP - 1)], recv_sem.at[0])
    for s in range(1, PER_CHUNK // EXP):
        wait_bytes(recv.at[pl.ds(s * EXP, EXP)], recv_sem.at[s])

    lane128 = lax.broadcasted_iota(I32, (CHUNK_ROWS, 128), 1)
    slot128 = lax.broadcasted_iota(I32, (CHUNK_ROWS, 128), 0) % CAP

    def give_back(j, k, xo):
        pltpu.make_async_remote_copy(
            src_ref=bsend.at[j],
            dst_ref=brecv.at[j],
            send_sem=bsend_sem,
            recv_sem=brecv_sem,
            device_id=behind(k, xo),
            device_id_type=MESH,
        ).start()
        pltpu.make_async_remote_copy(
            src_ref=hsend.at[j],
            dst_ref=hrecv.at[j],
            send_sem=hsend_sem,
            recv_sem=hrecv_sem,
            device_id=behind(k, xo),
            device_id_type=MESH,
        ).start()

    @pl.loop(0, CHUNKS)
    def _(ch):
        base = ch * PER_CHUNK

        @pl.when(ch > 0)
        def _():
            for i in range(PER_CHUNK // EXP):
                wait_bytes(
                    recv.at[pl.ds(base + i * EXP, EXP)], recv_sem.at[ch * (PER_CHUNK // EXP) + i]
                )

        rows = pl.ds(pl.multiple_of(ch * CHUNK_ROWS, CHUNK_ROWS), CHUNK_ROWS)
        peers = pl.ds(base, PER_CHUNK)
        came = recv[peers].astype(F32)
        u_all[rows] = came[:, :CAP].reshape(CHUNK_ROWS, WIDTH).astype(BF)
        s_all[rows] = came[:, CAP:].reshape(CHUNK_ROWS, WIDTH).astype(BF)

        def hidden(t, total):
            cols = pl.ds(pl.multiple_of(t * 256, 256), 256)
            pre = dot(u_all[rows], win[:, cols], 1, 0)
            grad = dot(s_all[rows], wout[cols, :], 1, 1)
            sigma = jax.nn.sigmoid(pre)
            act = pre * sigma
            act_all[rows, cols] = act.astype(BF)
            gp_all[rows, cols] = (grad * sigma * (1.0 + pre * (1.0 - sigma))).astype(BF)
            return total + jnp.sum(act * grad, axis=1, keepdims=True)

        total = lax.fori_loop(0, WIDTH // 256, hidden, jnp.zeros((CHUNK_ROWS, 1), F32))
        spread = jnp.where(lane128 == slot128, total, 0.0)
        hsend[peers] = jnp.sum(spread.reshape(PER_CHUNK, CAP, 128), axis=1, keepdims=True)

        @pl.loop(0, 2)
        def _(t):
            lo = pl.ds(pl.multiple_of(t * 256, 256), 256)
            hi = pl.ds(pl.multiple_of(t * 256 + 512, 256), 256)
            low = dot(gp_all[rows], win[lo, :], 1, 1).reshape(PER_CHUNK, CAP, 256)
            high = dot(gp_all[rows], win[hi, :], 1, 1).reshape(PER_CHUNK, CAP, 256)
            bsend[peers, :, lo] = jnp.concatenate([low, high], axis=1).astype(BF)

        @pl.when(ch == 0)
        def _():
            brecv[0] = bsend[0]
            hrecv[0] = hsend[0]
            for j in range(1, EXP):
                give_back(j, 0, j)

        @pl.when(ch > 0)
        def _():
            for i in range(EXP):
                give_back(base + i, *hop(base + i))

        @pl.loop(EXP, PER_CHUNK)
        def _(i):
            give_back(base + i, *hop(base + i))

    def make_part(o):
        cols = pl.ds(pl.multiple_of(lax.rem(me_d + o, DP) * PART, PART), PART)

        @pl.loop(0, 2)
        def _(t):
            half = pl.ds(pl.multiple_of(t * 512, 512), 512)
            part[o, 0, :, half] = dot(u_all[:, cols], gp_all[:, half], 0, 0).astype(BF)
            part[o, 1, :, half] = dot(act_all[:, cols], s_all[:, half], 0, 0).astype(BF)

    def to_dp(n, src, dst, other):
        copy = pltpu.make_async_remote_copy(
            src_ref=src,
            dst_ref=dst,
            send_sem=dp_send.at[n],
            recv_sem=dp_recv.at[n],
            device_id={"dp": other},
            device_id_type=MESH,
        )
        copy.start()
        return copy

    make_part(2)
    c0 = to_dp(0, part.at[2, 0], first.at[0], right)
    c1 = to_dp(1, part.at[2, 1], first.at[1], left)
    make_part(1)
    c2 = to_dp(2, part.at[1, 1], second.at[0, 1], right)
    make_part(3)
    c3 = to_dp(3, part.at[3, 0], second.at[1, 0], left)
    make_part(0)
    c0.wait_recv()
    part[1, 0] = (part[1, 0].astype(F32) + first[0].astype(F32)).astype(BF)
    c4 = to_dp(4, part.at[1, 0], second.at[0, 0], right)
    c1.wait_recv()
    part[3, 1] = (part[3, 1].astype(F32) + first[1].astype(F32)).astype(BF)
    c5 = to_dp(5, part.at[3, 1], second.at[1, 1], left)

    others = pl.ds(1, PEERS - 1)
    wait_bytes(brecv.at[others], brecv_sem)
    wait_bytes(hrecv.at[others], hrecv_sem)
    back = brecv[...].reshape(PEERS * BLOCK, WIDTH // 2)
    dres_ref[:, : WIDTH // 2] = (
        z_ref[:, : WIDTH // 2].astype(F32) + dot(pick_lo[...], back, 1, 0)
    ).astype(BF)
    dres_ref[:, WIDTH // 2 :] = (
        z_ref[:, WIDTH // 2 :].astype(F32) + dot(pick_hi[...], back, 1, 0)
    ).astype(BF)
    sums = jnp.sum(hrecv[...], axis=1)
    lane_s = lax.broadcasted_iota(I32, (TOKENS, 128), 1)
    parts = []
    for t in range(2):
        chosen = dot(named[t], sums, 1, 0, lax.Precision.HIGHEST)
        value = jnp.sum(jnp.where(lane_s == slot[t], chosen, 0.0), axis=1, keepdims=True)
        parts.append(value / gates[:, t : t + 1])
    lane2 = lax.broadcasted_iota(I32, (TOKENS, 2), 1)
    dgate_ref[...] = jnp.where(lane2 == 0, parts[0], parts[1]).astype(BF)

    for c in (c2, c3, c4, c5):
        c.wait_recv()
    for i in range(2):
        quarter_ref[i] = (
            part[0, i].astype(F32) + second[0, i].astype(F32) + second[1, i].astype(F32)
        ).astype(BF)
    for c in (c0, c1, c2, c3, c4, c5):
        c.wait_send()
    wait_bytes(send.at[others], send_sem)
    wait_bytes(bsend.at[others], bsend_sem)
    wait_bytes(hsend.at[others], hsend_sem)


def expert_layer(x, z, ids, gates, win, wout):
    vmem = pl.BlockSpec(memory_space=pltpu.VMEM)
    anywhere = pl.BlockSpec(memory_space=pl.ANY)
    rows = PEERS * CAP
    return pl.pallas_call(
        moe_kernel,
        out_shape=(
            jax.ShapeDtypeStruct((TOKENS, WIDTH), BF),
            jax.ShapeDtypeStruct((TOKENS, 2), BF),
            jax.ShapeDtypeStruct((2, PART, WIDTH), BF),
        ),
        in_specs=[vmem] * 4 + [anywhere] * 2,
        out_specs=(vmem,) * 3,
        scratch_shapes=[
            pltpu.VMEM((WIDTH, WIDTH), BF),
            pltpu.VMEM((WIDTH, WIDTH), BF),
            pltpu.VMEM((PEERS, BLOCK, WIDTH), BF),
            pltpu.VMEM((PEERS, BLOCK, WIDTH), BF),
            pltpu.VMEM((TOKENS, PEERS * BLOCK), BF),
            pltpu.VMEM((TOKENS, PEERS * BLOCK), BF),
            pltpu.VMEM((rows, WIDTH), BF),
            pltpu.VMEM((rows, WIDTH), BF),
            pltpu.VMEM((rows, WIDTH), BF),
            pltpu.VMEM((rows, WIDTH), BF),
            pltpu.VMEM((PEERS, BLOCK, WIDTH // 2), BF),
            pltpu.VMEM((PEERS, BLOCK, WIDTH // 2), BF),
            pltpu.VMEM((PEERS, 1, 128), F32),
            pltpu.VMEM((PEERS, 1, 128), F32),
            pltpu.VMEM((DP, 2, PART, WIDTH), BF),
            pltpu.VMEM((2, PART, WIDTH), BF),
            pltpu.VMEM((2, 2, PART, WIDTH), BF),
            pltpu.SemaphoreType.DMA((2,)),
            pltpu.SemaphoreType.DMA,
            pltpu.SemaphoreType.DMA((CTX,)),
            pltpu.SemaphoreType.DMA,
            pltpu.SemaphoreType.DMA,
            pltpu.SemaphoreType.DMA,
            pltpu.SemaphoreType.DMA,
            pltpu.SemaphoreType.DMA((6,)),
            pltpu.SemaphoreType.DMA((6,)),
        ],
        compiler_params=pltpu.CompilerParams(
            collective_id=0, has_side_effects=True, vmem_limit_bytes=VMEM_BYTES
        ),
        name="experts",
    )(x, z, ids, gates, win, wout)


def attention_kernel(
    q_ref,
    k_ref,
    v_ref,
    seg_ref,
    list_ref,
    dres_ref,
    quarter_ref,
    dq_ref,
    dk_ref,
    dv_ref,
    gin_ref,
    gout_ref,
    k_all,
    v_all,
    seg_prev,
    do_all,
    k_aug,
    q_aug,
    acc_k,
    acc_v,
    over,
    came,
    kv_send,
    kv_recv,
    do_send,
    do_recv,
    ag_send,
    ag_recv,
    own_sem,
    ret_send,
    ret_recv,
):
    me_d, me_c, me_x = lax.axis_index("dp"), lax.axis_index("ctx"), lax.axis_index("exp")
    right, left = lax.rem(me_d + 1, DP), lax.rem(me_d + DP - 1, DP)
    after, prior = lax.rem(me_c + 1, CTX), lax.rem(me_c + CTX - 1, CTX)

    barrier = pltpu.get_barrier_semaphore()
    for target in (
        [{"dp": left}, {"dp": right}, {"ctx": after}, {"ctx": prior}]
        + [{"exp": lax.rem(me_x + o, EXP)} for o in range(1, EXP)]
    ):
        pl.semaphore_signal(barrier, inc=1, device_id=target, device_id_type=MESH)
    pl.semaphore_wait(barrier, 4 + EXP - 1)

    def remote(src, dst, ssem, rsem, target):
        copy = pltpu.make_async_remote_copy(
            src_ref=src, dst_ref=dst, send_sem=ssem, recv_sem=rsem,
            device_id=target, device_id_type=MESH,
        )
        copy.start()
        return copy

    mine = pl.ds(pl.multiple_of(me_d * PART, PART), PART)
    lefts = pl.ds(pl.multiple_of(left * PART, PART), PART)
    rights = pl.ds(pl.multiple_of(right * PART, PART), PART)
    sends = []
    my_rows = pl.ds(pl.multiple_of(me_x * TOKENS, TOKENS), TOKENS)
    do_copies = []
    for o in range(1, EXP):
        px = lax.rem(me_x + o, EXP)
        do_copies.append(
            remote(
                dres_ref.at[:, pl.ds(pl.multiple_of(px * LOCAL, LOCAL), LOCAL)],
                do_all.at[my_rows],
                do_send.at[o - 1],
                do_recv.at[o - 1],
                {"exp": px},
            )
        )
    kv_copies = [
        remote(seg_ref, seg_prev, kv_send.at[2], kv_recv.at[2], {"ctx": after}),
        remote(k_ref, k_all.at[pl.ds(0, FRAMES)], kv_send.at[0], kv_recv.at[0], {"ctx": after}),
        remote(v_ref, v_all.at[pl.ds(0, FRAMES)], kv_send.at[1], kv_recv.at[1], {"ctx": after}),
    ]
    in_right = remote(
        quarter_ref.at[0], gin_ref.at[mine], ag_send.at[0], ag_recv.at[0], {"dp": right}
    )
    out_left = remote(
        quarter_ref.at[1], gout_ref.at[mine], ag_send.at[1], ag_recv.at[1], {"dp": left}
    )
    out_right = remote(
        quarter_ref.at[1], gout_ref.at[mine], ag_send.at[2], ag_recv.at[2], {"dp": right}
    )
    in_left = remote(
        quarter_ref.at[0], gin_ref.at[mine], ag_send.at[3], ag_recv.at[3], {"dp": left}
    )
    own = [
        pltpu.make_async_copy(quarter_ref.at[0], gin_ref.at[mine], own_sem.at[0]),
        pltpu.make_async_copy(quarter_ref.at[1], gout_ref.at[mine], own_sem.at[1]),
    ]
    for c in own:
        c.start()

    k_all[FRAMES:] = k_ref[...]
    v_all[FRAMES:] = v_ref[...]
    do_all[my_rows] = dres_ref[:, pl.ds(pl.multiple_of(me_x * LOCAL, LOCAL), LOCAL)]
    acc_k[...] = jnp.zeros_like(acc_k)
    acc_v[...] = jnp.zeros_like(acc_v)

    kinds = 2 * GROUPS
    lane_f = lax.broadcasted_iota(I32, (kinds, 128), 1)
    row_f = lax.broadcasted_iota(I32, (kinds, 128), 0)
    place = ((lane_f == row_f) | (lane_f == row_f + 64)).astype(F32).astype(BF)
    row8 = lax.broadcasted_iota(I32, (8, FRAMES), 0)
    group_of = lax.broadcasted_iota(I32, (8, FRAMES), 1) // GROUP
    seg_own = seg_ref[...] == row8
    kv_copies[0].wait_recv()
    seg_past = seg_prev[...] == row8
    lists = list_ref[...]
    moved = jnp.where(lists >= 0, lists - (me_c - 1) * GROUPS, -1)

    def listed(groups):
        return (
            (moved[:, 0:1] == groups) | (moved[:, 1:2] == groups) | (moved[:, 2:3] == groups)
        )

    list_past = listed(group_of)
    list_own = listed(group_of + GROUPS) | (group_of == row8)

    def features(segment, group, miss, match):
        both = jnp.concatenate(
            [jnp.where(segment, match, miss), jnp.where(group, match, miss)], axis=0
        ).astype(BF)
        return dot(both, place, 0, 0).astype(BF)

    feat_q = features(seg_own, group_of == row8, 0.0, 1.0)
    feat_past = features(seg_past, list_past, -FAR, 0.0)
    feat_own = features(seg_own, list_own, -FAR, 0.0)
    low = lax.broadcasted_iota(I32, (FRAMES, 128), 1) < 64
    for hp in range(2):
        tile = slice(hp * 128, hp * 128 + 128)
        q_t = (q_ref[:, tile].astype(F32) * 0.125).astype(BF)
        k_t = k_ref[:, tile]
        q_aug[2 * hp] = jnp.where(low, q_t, feat_q)
        q_aug[2 * hp + 1] = jnp.where(low, feat_q, q_t)
        k_aug[2 * hp, FRAMES:] = jnp.where(low, k_t, feat_own)
        k_aug[2 * hp + 1, FRAMES:] = jnp.where(low, feat_own, k_t)
    kv_copies[1].wait_recv()
    for hp in range(2):
        tile = slice(hp * 128, hp * 128 + 128)
        k_t = k_all[:FRAMES, tile]
        k_aug[2 * hp, :FRAMES] = jnp.where(low, k_t, feat_past)
        k_aug[2 * hp + 1, :FRAMES] = jnp.where(low, feat_past, k_t)
    kv_copies[2].wait_recv()
    for c in do_copies:
        c.wait_recv()

    low_q = lax.broadcasted_iota(I32, (QROWS, 128), 1) < 64
    none = jnp.zeros((QROWS, 128), BF)

    def block(b, carry):
        rows = pl.ds(pl.multiple_of(b * QROWS, QROWS), QROWS)
        window = pl.ds(pl.multiple_of(b * QROWS, QROWS), WINDOW)
        for hp in range(2):
            tile = slice(hp * 128, hp * 128 + 128)
            do_t = do_all[rows, tile]
            v_t = v_all[window, tile]
            k_t = k_all[window, tile]
            halves_p, halves_s, halves_d, halves_q, outs = [], [], [], [], []
            for e in range(2):
                q_a = q_aug[2 * hp + e, rows]
                score = dot(q_a, k_aug[2 * hp + e, window], 1, 1)
                high = jnp.max(score, axis=1, keepdims=True)
                weight = jnp.exp(score - high)
                weight = weight * (1.0 / jnp.sum(weight, axis=1, keepdims=True))
                probs = weight.astype(BF)
                keep = low_q if e == 0 else jnp.logical_not(low_q)
                do_e = jnp.where(keep, do_t, none)
                grad = dot(do_e, v_t, 1, 1)
                delta = jnp.sum(probs.astype(F32) * grad, axis=1, keepdims=True)
                dscore = (weight * (grad - delta)).astype(BF)
                outs.append(dot(dscore, k_t, 1, 0))
                halves_p.append(probs)
                halves_s.append(dscore)
                halves_d.append(do_e)
                halves_q.append(jnp.where(keep, q_a, none))
            dq_ref[rows, tile] = (jnp.where(low_q, outs[0], outs[1]) * 0.125).astype(BF)
            acc_k[window, tile] += dot(
                jnp.concatenate(halves_s, axis=0), jnp.concatenate(halves_q, axis=0), 0, 0
            )
            acc_v[window, tile] += dot(
                jnp.concatenate(halves_p, axis=0), jnp.concatenate(halves_d, axis=0), 0, 0
            )
        return carry

    blocks = FRAMES // QROWS
    lax.fori_loop(0, blocks // 2, block, 0)
    in_right.wait_recv()
    on_right = remote(
        gin_ref.at[lefts], gin_ref.at[lefts], ag_send.at[4], ag_recv.at[4], {"dp": right}
    )
    out_left.wait_recv()
    on_left = remote(
        gout_ref.at[rights], gout_ref.at[rights], ag_send.at[5], ag_recv.at[5], {"dp": left}
    )
    lax.fori_loop(blocks // 2, blocks, block, 0)

    over[0] = acc_k[:FRAMES].astype(BF)
    over[1] = acc_v[:FRAMES].astype(BF)
    returned = [
        remote(over.at[i], came.at[i], ret_send.at[i], ret_recv.at[i], {"ctx": prior})
        for i in range(2)
    ]
    returned[0].wait_recv()
    dk_ref[...] = (acc_k[FRAMES:] + came[0].astype(F32)).astype(BF)
    returned[1].wait_recv()
    dv_ref[...] = (acc_v[FRAMES:] + came[1].astype(F32)).astype(BF)
    for c in (out_right, in_left, on_right, on_left):
        c.wait_recv()
    for c in own:
        c.wait()
    for c in do_copies + kv_copies + returned:
        c.wait_send()
    for c in (in_right, out_left, out_right, in_left, on_right, on_left):
        c.wait_send()


def attention(q, k, v, seg, lists, dres, quarter):
    vmem = pl.BlockSpec(memory_space=pltpu.VMEM)
    anywhere = pl.BlockSpec(memory_space=pl.ANY)
    frames = jax.ShapeDtypeStruct((FRAMES, LOCAL), BF)
    weight = jax.ShapeDtypeStruct((WIDTH, WIDTH), BF)
    dma = pltpu.SemaphoreType.DMA
    return pl.pallas_call(
        attention_kernel,
        out_shape=(frames, frames, frames, weight, weight),
        in_specs=[vmem] * 7,
        out_specs=(vmem, vmem, vmem, anywhere, anywhere),
        scratch_shapes=[
            pltpu.VMEM((2 * FRAMES, LOCAL), BF),
            pltpu.VMEM((2 * FRAMES, LOCAL), BF),
            pltpu.VMEM((1, FRAMES), I32),
            pltpu.VMEM((FRAMES, LOCAL), BF),
            pltpu.VMEM((4, 2 * FRAMES, 128), BF),
            pltpu.VMEM((4, FRAMES, 128), BF),
            pltpu.VMEM((2 * FRAMES, LOCAL), F32),
            pltpu.VMEM((2 * FRAMES, LOCAL), F32),
            pltpu.VMEM((2, FRAMES, LOCAL), BF),
            pltpu.VMEM((2, FRAMES, LOCAL), BF),
            dma((3,)),
            dma((3,)),
            dma((3,)),
            dma((3,)),
            dma((6,)),
            dma((6,)),
            dma((2,)),
            dma((2,)),
            dma((2,)),
        ],
        compiler_params=pltpu.CompilerParams(
            collective_id=1, has_side_effects=True, vmem_limit_bytes=VMEM_BYTES
        ),
        name="attention",
    )(q, k, v, seg, lists, dres, quarter)


def local(
    queries,
    key_rows,
    value_rows,
    segments,
    left_blocks,
    moe_input,
    out_grad,
    expert_ids,
    gate_weights,
    expert_in,
    expert_out,
):
    d_residual, d_gates, quarter = expert_layer(
        moe_input[0], out_grad[0], expert_ids[0], gate_weights[0], expert_in[0], expert_out[0]
    )
    dq, dk, dv, grad_in, grad_out = attention(
        queries[0], key_rows[0], value_rows[0], segments, left_blocks[0], d_residual, quarter
    )
    return (
        dq[None],
        dk[None],
        dv[None],
        d_residual[None],
        d_gates[None],
        grad_in[None],
        grad_out[None],
    )


def solution(mesh):
    assert dict(mesh.shape) == {"dp": DP, "ctx": CTX, "exp": EXP}
    return jax.shard_map(
        local,
        mesh=mesh,
        in_specs=(
            P("dp", "ctx", "exp"),
            P("dp", "ctx", "exp"),
            P("dp", "ctx", "exp"),
            P("dp", "ctx"),
            P("dp", "ctx", None),
            P("dp", ("ctx", "exp"), None),
            P("dp", ("ctx", "exp"), None),
            P("dp", ("ctx", "exp"), None),
            P("dp", ("ctx", "exp"), None),
            P(("ctx", "exp"), None, None),
            P(("ctx", "exp"), None, None),
        ),
        out_specs=(
            P("dp", "ctx", "exp"),
            P("dp", "ctx", "exp"),
            P("dp", "ctx", "exp"),
            P("dp", ("ctx", "exp"), None),
            P("dp", ("ctx", "exp"), None),
            P(("ctx", "exp"), None, None),
            P(("ctx", "exp"), None, None),
        ),
        check_vma=False,
    )
```

time: 309 us -> 154 us (0.50); the launches traced: 305 us -> 154 us
  Pallas kernels: 0 us -> 141 us
  local copies, waits for them, and re-layouts: 83.9 us -> 12.9 us
  starting transfers between devices: 69.2 us -> 0 us
  waiting for transfers between devices: 54.1 us -> 0 us
  blocking collectives: 37.7 us -> 0 us
  matrix products: 31.1 us -> 0 us
  between operations: 15.2 us -> 0.68 us
  other arithmetic: 13.8 us -> 0 us
    pallas_call x0 -> x2, Pallas kernels: none -> 141 us  [the longest x1 103 us: expert_layer(): pl.pallas_call(moe_kernel, out_shape=(jax.ShapeDtypeStruct((TOKENS, WIDTH...]
    all_to_all x5 -> x0, starting transfers between devices: 54.5 us -> none  [the longest x1 21.5 us: local(): lax.all_to_all(gate_grad.reshape(experts, capacity), ('ctx', 'exp'), spli...]
    all_to_all x1 -> x0, blocking collectives: 37.7 us -> none  [local(): lax.all_to_all(rows_in, ('ctx', 'exp'), split_axis=0, concat_axis=0, tile...]
    psum x1 -> x0, waiting for transfers between devices: 32.1 us -> none  [local(): lax.psum(grad_in.astype(jnp.bfloat16), 'dp').astype(jnp.float32)]
    dot_general x14 -> x0, matrix products: 31.1 us -> none  [the longest x1 4.2 us: expert_backward(): lax.dot_general(scaled, weight_out, (((1,), (1,)), ((), ())), preferred_e...]
    gather x10 -> x0, local copies, waits for them, and re-layouts: 27.4 us -> none  [the longest x2 7.4 us: attention_grads(): key_blocks = key_all[local_index].reshape(n_groups, listed * CH, heads, DH)]
    reshape x10 -> x0, local copies, waits for them, and re-layouts: 21.5 us -> none  [the longest x1 4.66 us: attention_grads(): key_terms.reshape(n_groups, listed, CH * local_width)]
    ppermute x5 -> x0, starting transfers between devices: 14.6 us -> none  [from_behind(): return lax.ppermute(block, axis, route)]
  transfers between devices with their start and end apart: 11 -> 0, of which waited for: 7 -> 0; matrix products, arithmetic and copies ran while one was open for 36% -> 0% of each run, Pallas kernels for 0% -> 0%
where the time goes in v1:
time: 154 us
  Pallas kernels  141 us (92%)
  local copies, waits for them, and re-layouts  12.9 us (8%)
    pallas_call x1, Pallas kernels, expert_layer(): pl.pallas_call(moe_kernel, out_shape=(jax.ShapeDtypeStruct((TOKENS, WIDTH...  103 us
    pallas_call x1, Pallas kernels, attention(): pl.pallas_call(attention_kernel, out_shape=(frames, frames, frames, weigh...  37.4 us
    unnamed x27, local copies, waits for them, and re-layouts  12.2 us

profile of v1, /device:TPU:1, one launch (start us, length us, event | category | flops | bytes accessed | tf_op | source)
XLA Modules:
  0.0 154.2 jit_solution(6714088090538262340)
XLA Ops:
  0.6 0.8 copy.22
  1.4 0.8 copy.19
  2.2 0.8 copy.18
  3.0 0.0 copy-start
  3.0 1.6 %copy-done = bf16[1,1024,1024]{2,1,0:T(8,128)(2,1)S(1)} copy-done((bf16[1,1024,1024]{2,1,0:T(8,128)(2,1)S(1)}, bf16[1,1024,1024]{2,1,0:T(8,128)(2,1)}, u32[]{:S(2)}) %copy-start) | copy-done | bytes 2097176
  4.5 0.0 copy-start.1
  4.6 0.9 copy-done.1
  5.5 0.0 copy-start.2
  5.5 0.9 copy-done.2
  6.5 0.0 copy-start.3
  6.5 0.0 copy-start.4
  6.5 0.0 copy-start.5
  6.5 0.0 copy-start.6
  6.5 103.3 %experts.1 = (bf16[128,1024]{1,0:T(8,128)(2,1)S(1)}, bf16[128,2]{1,0:T(8,128)(2,1)S(1)}, bf16[2,256,1024]{2,1,0:T(8,128)(2,1)S(1)}) custom-call(bf16[128,1024]{1,0:T(8,128)(2,1)S(1)} %bitcast.20, bf16[128,1024]{1,0:T(8,128)(2,1)S(1)} %bitcast.21, s32[128,2]{1,0:T(8,128)S(1)} %bitcast.19, bf16[128,2]{1,0:T(8,128)(2,1)S(1)} %bitcast.28, ...), custom_call_target="tpu_custom_call" | custom-call | tf_op jit(solution)/shard_map/experts/pallas_call | solution.py:328
  109.8 0.6 copy.21
  110.4 0.0 copy-done.3
  110.4 0.0 copy-done.4
  110.4 0.0 copy-done.5
  110.4 0.0 copy-done.6
  110.4 37.4 %attention.1 = (bf16[512,256]{1,0:T(8,128)(2,1)S(1)}, bf16[512,256]{1,0:T(8,128)(2,1)S(1)}, bf16[512,256]{1,0:T(8,128)(2,1)S(1)}, bf16[1024,1024]{1,0:T(8,128)(2,1)}, bf16[1024,1024]{1,0:T(8,128)(2,1)}) custom-call(bf16[512,256]{1,0:T(8,128)(2,1)S(1)} %bitcast.22, bf16[512,256]{1,0:T(8,128)(2,1)S(1)} %bitcast.23, bf16[512,256]{1,0:T(8,128)(2,1)S(1)} %bitcast.24, ...), custom_call_target="tpu_custom_call" | custom-call | tf_op jit(solution)/shard_map/attention/pallas_call | solution.py:596
  147.7 0.0 copy-start.8
  147.8 0.7 copy.29
  148.5 0.7 copy.30
  149.2 0.7 copy.31
  149.9 0.7 copy.32
  150.6 0.0 copy-done.8
  150.6 0.0 copy-start.7
  150.6 1.3 copy.33
  151.9 1.0 copy-done.7
  152.9 1.3 copy.34
Async XLA Ops:
  3.0 1.6 %copy-start = (bf16[1,1024,1024]{2,1,0:T(8,128)(2,1)S(1)}, bf16[1,1024,1024]{2,1,0:T(8,128)(2,1)}, u32[]{:S(2)}) copy-start(bf16[1,1024,1024]{2,1,0:T(8,128)(2,1)} %param.20) | copy-start | bytes 6291460
  4.5 0.9 copy-start.1
  5.5 0.9 copy-start.2
  6.5 103.9 %copy-start.3 = (bf16[1,512,256]{2,1,0:T(8,128)(2,1)S(1)}, bf16[1,512,256]{2,1,0:T(8,128)(2,1)}, u32[]{:S(2)}) copy-start(bf16[1,512,256]{2,1,0:T(8,128)(2,1)} %param.11) | copy-start | bytes 786436
  6.5 103.9 %copy-start.4 = (bf16[1,512,256]{2,1,0:T(8,128)(2,1)S(1)}, bf16[1,512,256]{2,1,0:T(8,128)(2,1)}, u32[]{:S(2)}) copy-start(bf16[1,512,256]{2,1,0:T(8,128)(2,1)} %param.12) | copy-start | bytes 786436
  6.5 103.9 %copy-start.5 = (bf16[1,512,256]{2,1,0:T(8,128)(2,1)S(1)}, bf16[1,512,256]{2,1,0:T(8,128)(2,1)}, u32[]{:S(2)}) copy-start(bf16[1,512,256]{2,1,0:T(8,128)(2,1)} %param.13) | copy-start | bytes 786436
  6.5 103.9 %copy-start.6 = (s32[1,512]{1,0:T(1,128)S(1)}, s32[1,512]{1,0:T(1,128)}, u32[]{:S(2)}) copy-start(s32[1,512]{1,0:T(1,128)} %seg_ref.1) | copy-start | bytes 6148
  147.7 2.8 %copy-start.8 = (bf16[1024,1024]{1,0:T(8,128)(2,1)S(1)}, bf16[1024,1024]{1,0:T(8,128)(2,1)}, u32[]{:S(2)}) copy-start(bf16[1024,1024]{1,0:T(8,128)(2,1)} %get-tuple-element.21) | copy-start | bytes 6291460
  150.6 2.3 %copy-start.7 = (bf16[1024,1024]{1,0:T(8,128)(2,1)S(1)}, bf16[1024,1024]{1,0:T(8,128)(2,1)}, u32[]{:S(2)}) copy-start(bf16[1024,1024]{1,0:T(8,128)(2,1)} %get-tuple-element.22) | copy-start | bytes 6291460

commit v2 on v0

v2 whole, which is shorter than its diff:
```python
import types

import jax
import jax.numpy as jnp
from jax import lax
from jax.experimental import pallas as pl
from jax.experimental.pallas import tpu as pltpu
from jax.sharding import PartitionSpec as P

MESH = pl.DeviceIdType.MESH
BF = jnp.bfloat16
F32 = jnp.float32
I32 = jnp.int32

DP, CTX, EXP = 4, 16, 4
PEERS = CTX * EXP
HALF = CTX // 2
CAP = 8
BLOCK = 2 * CAP
TOKENS = 128
WIDTH = 1024
PART = WIDTH // DP
CHUNKS = 4
PER_CHUNK = PEERS // CHUNKS
CHUNK_ROWS = PER_CHUNK * CAP
ROWS = PEERS * CAP
ORDER = (2, 1, 3, 0)
GROUP = 64
GROUPS = 8
FRAMES = 512
LOCAL = 256
QROWS = 128
BLOCKS = FRAMES // QROWS
WINDOW = FRAMES + QROWS
FAR = 32768.0
VMEM_BYTES = 56 * 1024 * 1024


def dot(a, b, ca, cb, precision=None):
    return lax.dot_general(
        a, b, (((ca,), (cb,)), ((), ())), preferred_element_type=F32, precision=precision
    )


def wait_bytes(ref, sem):
    pltpu.make_async_copy(ref, ref, sem).wait()


def span(index, size):
    return pl.ds(pl.multiple_of(index * size, size), size)


def hop(j):
    s = j // EXP
    return HALF + (2 * (s % 2) - 1) * (s // 2), j % EXP


def iota(shape, dim):
    return lax.broadcasted_iota(I32, shape, dim)


def column(row):
    n = row.shape[1]
    same = iota((n, n), 0) == iota((n, n), 1)
    return jnp.sum(jnp.where(same, row, jnp.zeros_like(row)), axis=1, keepdims=True)


def as_row(col):
    n = col.shape[0]
    same = iota((n, n), 0) == iota((n, n), 1)
    return jnp.sum(jnp.where(same, col, jnp.zeros_like(col)), axis=0, keepdims=True)


INPUTS = ("q", "k", "v", "seg", "lists", "x", "z", "ids", "gate", "win", "wout")
OUTPUTS = ("dq", "dk", "dv", "dres", "dgate", "gout", "gin")
DMA = pltpu.SemaphoreType.DMA
LOADS = ("ids", "gate", "x", "z", "win", "wout", "q", "seg", "lists", "k", "v")
SCRATCH = dict(
    q_own=pltpu.VMEM((FRAMES, LOCAL), BF),
    seg_own=pltpu.VMEM((1, FRAMES), I32),
    lists_own=pltpu.VMEM((3, 1, GROUPS), I32),
    x_own=pltpu.VMEM((TOKENS, WIDTH), BF),
    z_own=pltpu.VMEM((TOKENS, WIDTH), BF),
    ids_own=pltpu.VMEM((2, TOKENS), I32),
    gate_own=pltpu.VMEM((2, TOKENS), BF),
    w_in=pltpu.VMEM((WIDTH, WIDTH), BF),
    w_out=pltpu.VMEM((WIDTH, WIDTH), BF),
    pick=pltpu.VMEM((2 * TOKENS, PEERS * BLOCK), BF),
    gated=pltpu.VMEM((2 * TOKENS, PEERS * BLOCK), BF),
    xx=pltpu.VMEM((2 * TOKENS, WIDTH // 2), BF),
    zz=pltpu.VMEM((2 * TOKENS, WIDTH // 2), BF),
    send_u=pltpu.VMEM((PEERS, BLOCK, WIDTH // 2), BF),
    recv_u=pltpu.VMEM((PEERS, BLOCK, WIDTH // 2), BF),
    send_s=pltpu.VMEM((DP, PEERS, BLOCK, PART // 2), BF),
    recv_s=pltpu.VMEM((DP, PEERS, BLOCK, PART // 2), BF),
    u_chunk=pltpu.VMEM((CHUNK_ROWS, WIDTH), BF),
    u_t=pltpu.VMEM((WIDTH, ROWS), BF),
    act_t=pltpu.VMEM((WIDTH, ROWS), BF),
    pre_all=pltpu.VMEM((ROWS, WIDTH), F32),
    s_all=pltpu.VMEM((ROWS, WIDTH), BF),
    gp_all=pltpu.VMEM((ROWS, WIDTH), BF),
    bsend=pltpu.VMEM((PEERS, BLOCK, WIDTH // 2), BF),
    brecv=pltpu.VMEM((PEERS, BLOCK, WIDTH // 2), BF),
    hsend=pltpu.VMEM((PEERS, 1, 128), F32),
    hrecv=pltpu.VMEM((PEERS, 1, 128), F32),
    part=pltpu.VMEM((2, DP, WIDTH, PART), BF),
    first=pltpu.VMEM((2, 2, WIDTH // 2, PART), BF),
    second=pltpu.VMEM((2, 2, WIDTH, PART), BF),
    fin=pltpu.VMEM((2, WIDTH, PART), BF),
    k_all=pltpu.VMEM((2 * FRAMES, LOCAL), BF),
    v_all=pltpu.VMEM((2 * FRAMES, LOCAL), BF),
    seg_prev=pltpu.VMEM((1, FRAMES), I32),
    do_all=pltpu.VMEM((FRAMES, LOCAL), BF),
    k_aug=pltpu.VMEM((4, 2 * FRAMES, 128), BF),
    q_aug=pltpu.VMEM((4, FRAMES, 128), BF),
    probs=pltpu.VMEM((4, FRAMES, WINDOW), BF),
    acc_k=pltpu.VMEM((2 * FRAMES, LOCAL), F32),
    acc_v=pltpu.VMEM((2 * FRAMES, LOCAL), F32),
    over=pltpu.VMEM((2, FRAMES, LOCAL), BF),
    came=pltpu.VMEM((2, FRAMES, LOCAL), BF),
    load_sem=DMA((len(LOADS),)),
    u_send=DMA,
    u_recv=DMA((CTX,)),
    s_send=DMA((DP,)),
    s_recv=DMA((DP,)),
    b_send=DMA,
    b_recv=DMA,
    h_send=DMA,
    h_recv=DMA,
    rs_send=DMA((2, 6)),
    rs_recv=DMA((2, 6)),
    ag_send=DMA((2, 6)),
    ag_recv=DMA((2, 6)),
    own_sem=DMA((2,)),
    kv_send=DMA((3,)),
    kv_recv=DMA((3,)),
    do_send=DMA((EXP - 1,)),
    do_recv=DMA((EXP - 1,)),
    ret_send=DMA((2,)),
    ret_recv=DMA((2,)),
)


def layer_kernel(*refs):
    r = types.SimpleNamespace(**dict(zip(INPUTS + OUTPUTS + tuple(SCRATCH), refs)))
    me_d, me_c, me_x = lax.axis_index("dp"), lax.axis_index("ctx"), lax.axis_index("exp")
    right, left = lax.rem(me_d + 1, DP), lax.rem(me_d + DP - 1, DP)
    after, prior = lax.rem(me_c + 1, CTX), lax.rem(me_c + CTX - 1, CTX)
    outs = (r.gout, r.gin)

    targets = dict(
        ids=r.ids_own,
        gate=r.gate_own,
        x=r.x_own,
        z=r.z_own,
        win=r.w_in,
        wout=r.w_out,
        q=r.q_own,
        seg=r.seg_own,
        lists=r.lists_own,
        k=r.k_all.at[pl.ds(FRAMES, FRAMES)],
        v=r.v_all.at[pl.ds(FRAMES, FRAMES)],
    )
    loads = {
        name: pltpu.make_async_copy(getattr(r, name), targets[name], r.load_sem.at[i])
        for i, name in enumerate(LOADS)
    }
    for name in LOADS:
        loads[name].start()

    def ahead(k, xo):
        return {"ctx": lax.rem(me_c + k, CTX), "exp": lax.rem(me_x + xo, EXP)}

    def behind(k, xo):
        return {"ctx": lax.rem(me_c - k + CTX, CTX), "exp": lax.rem(me_x - xo + EXP, EXP)}

    def remote(src, dst, ssem, rsem, target):
        copy = pltpu.make_async_remote_copy(
            src_ref=src,
            dst_ref=dst,
            send_sem=ssem,
            recv_sem=rsem,
            device_id=target,
            device_id_type=MESH,
        )
        copy.start()
        return copy

    barrier = pltpu.get_barrier_semaphore()
    for other in (left, right):
        pl.semaphore_signal(barrier, inc=1, device_id={"dp": other}, device_id_type=MESH)
    for j in range(1, EXP):
        pl.semaphore_signal(barrier, inc=1, device_id=ahead(0, j), device_id_type=MESH)

    @pl.loop(EXP, PEERS)
    def _(j):
        k, xo = hop(j)
        pl.semaphore_signal(barrier, inc=1, device_id=ahead(k, xo), device_id_type=MESH)

    lane64 = iota((TOKENS, PEERS), 1)
    lane_q = iota((TOKENS, PEERS * BLOCK), 1)

    def relative(ids):
        k = (ids // EXP - me_c + CTX) % CTX
        xo = (ids % EXP - me_x + EXP) % EXP
        s = jnp.where(k == 0, 0, jnp.where(k < HALF, CTX - 2 * k, 2 * k - CTX + 1))
        return s * EXP + xo

    loads["ids"].wait()
    peer = [column(relative(r.ids_own[t : t + 1, :])) for t in range(2)]
    named = [(peer[t] == lane64).astype(F32) for t in range(2)]
    before = (iota((TOKENS, TOKENS), 1) < iota((TOKENS, TOKENS), 0)).astype(F32).astype(BF)
    earlier = dot(before, (named[0] + named[1]).astype(BF), 1, 0)
    slot = [jnp.sum(named[t] * earlier, axis=1, keepdims=True).astype(I32) for t in range(2)]
    row = [peer[t] * BLOCK + slot[t] for t in range(2)]
    loads["gate"].wait()
    gates = [column(r.gate_own[t : t + 1, :].astype(F32)) for t in range(2)]
    for half in range(2):
        hit = [row[t] + half * CAP == lane_q for t in range(2)]
        rows = pl.ds(half * TOKENS, TOKENS)
        r.pick[rows] = (hit[0] | hit[1]).astype(F32).astype(BF)
        r.gated[rows] = (
            jnp.where(hit[0], gates[0], 0.0) + jnp.where(hit[1], gates[1], 0.0)
        ).astype(BF)
    loads["x"].wait()
    r.xx[:TOKENS] = r.x_own[:, : WIDTH // 2]
    r.xx[TOKENS:] = r.x_own[:, WIDTH // 2 :]

    @pl.loop(0, CHUNKS)
    def _(t):
        rows = dot(r.pick[:, span(t, 256)], r.xx[...], 0, 0)
        r.send_u[pl.ds(t * 16, 16)] = rows.astype(BF).reshape(16, BLOCK, WIDTH // 2)

    pl.semaphore_wait(barrier, PEERS - 1 + 2)

    def send_rows(j, k, xo):
        remote(r.send_u.at[j], r.recv_u.at[j], r.u_send, r.u_recv.at[j // EXP], ahead(k, xo))

    @pl.loop(EXP, PEERS)
    def _(j):
        send_rows(j, *hop(j))

    for j in range(1, EXP):
        send_rows(j, 0, j)
    r.recv_u[0] = r.send_u[0]

    loads["z"].wait()
    for n, o in enumerate(ORDER):
        member = lax.rem(me_d + o, DP)
        tile = slice(n * 128, n * 128 + 128)
        r.zz[:TOKENS, tile] = r.z_own[:, span(2 * member, 128)]
        r.zz[TOKENS:, tile] = r.z_own[:, span(2 * member + 1, 128)]

    @pl.loop(0, CHUNKS)
    def _(t):
        rows = dot(r.gated[:, span(t, 256)], r.zz[...], 0, 0).astype(BF)
        for n in range(DP):
            r.send_s[n, pl.ds(t * 16, 16)] = rows[:, n * 128 : n * 128 + 128].reshape(
                16, BLOCK, 128
            )

    for n in range(DP):

        def send_grads(j, k, xo):
            remote(
                r.send_s.at[n, j], r.recv_s.at[n, j], r.s_send.at[n], r.s_recv.at[n], ahead(k, xo)
            )

        @pl.loop(EXP, PEERS)
        def _(j):
            send_grads(j, *hop(j))

        for j in range(1, EXP):
            send_grads(j, 0, j)
        r.recv_s[n, 0] = r.send_s[n, 0]

    past = pl.ds(0, FRAMES)
    kv_copies = [
        remote(r.seg, r.seg_prev, r.kv_send.at[0], r.kv_recv.at[0], {"ctx": after}),
        remote(r.k, r.k_all.at[past], r.kv_send.at[1], r.kv_recv.at[1], {"ctx": after}),
        remote(r.v, r.v_all.at[past], r.kv_send.at[2], r.kv_recv.at[2], {"ctx": after}),
    ]

    for name in ("q", "seg", "lists", "k", "v"):
        loads[name].wait()
    kinds = 2 * GROUPS
    lane_f, row_f = iota((kinds, 128), 1), iota((kinds, 128), 0)
    place = ((lane_f == row_f) | (lane_f == row_f + 64)).astype(F32).astype(BF)
    row8 = iota((8, FRAMES), 0)
    group_of = iota((8, FRAMES), 1) // GROUP
    moved = []
    for j in range(3):
        lists = column(r.lists_own[j])
        moved.append(jnp.where(lists >= 0, lists - (me_c - 1) * GROUPS, -1))

    def listed(groups):
        return (moved[0] == groups) | (moved[1] == groups) | (moved[2] == groups)

    def features(segment, group, miss, match):
        both = jnp.concatenate(
            [jnp.where(segment, match, miss), jnp.where(group, match, miss)], axis=0
        ).astype(BF)
        return dot(both, place, 0, 0).astype(BF)

    low = iota((FRAMES, 128), 1) < 64
    low_q = iota((QROWS, 128), 1) < 64
    none = jnp.zeros((QROWS, 128), BF)

    def augment(part, feat):
        for hp in range(2):
            k_t = r.k_all[part, hp * 128 : hp * 128 + 128]
            r.k_aug[2 * hp, part] = jnp.where(low, k_t, feat)
            r.k_aug[2 * hp + 1, part] = jnp.where(low, feat, k_t)

    seg_own = r.seg_own[...] == row8
    feat_q = features(seg_own, group_of == row8, 0.0, 1.0)
    for hp in range(2):
        q_t = (r.q_own[:, hp * 128 : hp * 128 + 128].astype(F32) * 0.125).astype(BF)
        r.q_aug[2 * hp] = jnp.where(low, q_t, feat_q)
        r.q_aug[2 * hp + 1] = jnp.where(low, feat_q, q_t)
    list_own = listed(group_of + GROUPS) | (group_of == row8)
    augment(pl.ds(FRAMES, FRAMES), features(seg_own, list_own, -FAR, 0.0))
    r.acc_k[...] = jnp.zeros_like(r.acc_k)
    r.acc_v[...] = jnp.zeros_like(r.acc_v)

    loads["win"].wait()
    loads["wout"].wait()

    @pl.loop(0, CHUNKS)
    def _(ch):
        base = ch * PER_CHUNK

        @pl.when(ch == 0)
        def _():
            wait_bytes(r.recv_u.at[pl.ds(1, EXP - 1)], r.u_recv.at[0])

        @pl.when(ch > 0)
        def _():
            wait_bytes(r.recv_u.at[pl.ds(base, EXP)], r.u_recv.at[ch * (PER_CHUNK // EXP)])

        for i in range(1, PER_CHUNK // EXP):
            wait_bytes(
                r.recv_u.at[pl.ds(base + i * EXP, EXP)], r.u_recv.at[ch * (PER_CHUNK // EXP) + i]
            )
        rows = span(ch, CHUNK_ROWS)
        came = r.recv_u[pl.ds(base, PER_CHUNK)].astype(F32)
        for half in range(2):
            cols = slice(half * 512, half * 512 + 512)
            u = came[:, half * CAP : half * CAP + CAP].reshape(CHUNK_ROWS, WIDTH // 2)
            r.u_chunk[:, cols] = u.astype(BF)
            r.u_t[cols, rows] = u.T.astype(BF)

        @pl.loop(0, WIDTH // 256)
        def _(t):
            cols = span(t, 256)
            pre = dot(r.u_chunk[...], r.w_in[:, cols], 1, 0)
            r.pre_all[rows, cols] = pre
            r.act_t[cols, rows] = (pre * jax.nn.sigmoid(pre)).T.astype(BF)

    top, bottom = pl.ds(0, WIDTH // 2), pl.ds(WIDTH // 2, WIDTH // 2)
    halves = (top, bottom)

    def reduce_send(a, n, src, dst, other):
        return remote(src, dst, r.rs_send.at[a, n], r.rs_recv.at[a, n], {"dp": other})

    def make_part(a, o, lhs, rhs):
        @pl.loop(0, 2)
        def _(t):
            rows = span(t, 512)
            r.part[a, o, rows] = dot(lhs[rows, :], rhs, 1, 0).astype(BF)

    reduces = [{}, {}]

    def reduce_direct(a, o):
        c = reduces[a]
        if o == 2:
            c[0] = reduce_send(a, 0, r.part.at[a, 2, top], r.first.at[a, 0], right)
            c[1] = reduce_send(a, 1, r.part.at[a, 2, bottom], r.first.at[a, 1], left)
        if o == 1:
            c[2] = reduce_send(a, 2, r.part.at[a, 1, bottom], r.second.at[a, 0, bottom], right)
        if o == 3:
            c[3] = reduce_send(a, 3, r.part.at[a, 3, top], r.second.at[a, 1, top], left)

    def reduce_relay(a, o):
        c = reduces[a]
        side, half, other = (0, top, right) if o == 1 else (1, bottom, left)
        c[side].wait_recv()
        r.part[a, o, half] = (
            r.part[a, o, half].astype(F32) + r.first[a, side].astype(F32)
        ).astype(BF)
        c[4 + side] = reduce_send(
            a, 4 + side, r.part.at[a, o, half], r.second.at[a, side, half], other
        )

    mine, lefts, rights = span(me_d, PART), span(left, PART), span(right, PART)
    gathers = [{}, {}]
    own = []

    def gather_send(a, n, src, where, other):
        rows, cols = where
        return remote(
            src, outs[a].at[rows, cols], r.ag_send.at[a, n], r.ag_recv.at[a, n], {"dp": other}
        )

    def reduce_end(a):
        for n in (2, 3, 4, 5):
            reduces[a][n].wait_recv()
        r.fin[a] = (
            r.part[a, 0].astype(F32) + r.second[a, 0].astype(F32) + r.second[a, 1].astype(F32)
        ).astype(BF)
        g = gathers[a]
        g[0] = gather_send(a, 0, r.fin.at[a, top], (top, mine), right)
        g[1] = gather_send(a, 1, r.fin.at[a, bottom], (bottom, mine), left)
        g[2] = gather_send(a, 2, r.fin.at[a, bottom], (bottom, mine), right)
        g[3] = gather_send(a, 3, r.fin.at[a, top], (top, mine), left)
        copy = pltpu.make_async_copy(r.fin.at[a], outs[a].at[:, mine], r.own_sem.at[a])
        copy.start()
        own.append(copy)

    def gather_on(a):
        g = gathers[a]
        g[0].wait_recv()
        g[4] = gather_send(a, 4, outs[a].at[top, lefts], (top, lefts), right)
        g[1].wait_recv()
        g[5] = gather_send(a, 5, outs[a].at[bottom, rights], (bottom, rights), left)

    others = pl.ds(1, PEERS - 1)
    for n, o in enumerate(ORDER):
        member = lax.rem(me_d + o, DP)
        wait_bytes(r.recv_s.at[n, others], r.s_recv.at[n])
        came = r.recv_s[n].astype(F32)
        for half in range(2):
            r.s_all[:, span(2 * member + half, 128)] = (
                came[:, half * CAP : half * CAP + CAP].reshape(ROWS, 128).astype(BF)
            )
        make_part(0, o, r.act_t, r.s_all[:, span(member, PART)])
        reduce_direct(0, o)
        if o in (1, 3):
            reduce_relay(0, o)

    lane128 = iota((CHUNK_ROWS, 128), 1)
    slot128 = iota((CHUNK_ROWS, 128), 0) % CAP

    def give_back(j, k, xo):
        remote(r.bsend.at[j], r.brecv.at[j], r.b_send, r.b_recv, behind(k, xo))
        remote(r.hsend.at[j], r.hrecv.at[j], r.h_send, r.h_recv, behind(k, xo))

    @pl.loop(0, CHUNKS)
    def _(ch):
        base = ch * PER_CHUNK
        rows = span(ch, CHUNK_ROWS)
        peers = pl.ds(base, PER_CHUNK)

        def hidden(t, total):
            cols = span(t, 256)
            grad = dot(r.s_all[rows], r.w_out[cols, :], 1, 1)
            pre = r.pre_all[rows, cols]
            sigma = jax.nn.sigmoid(pre)
            r.gp_all[rows, cols] = (grad * sigma * (1.0 + pre * (1.0 - sigma))).astype(BF)
            return total + jnp.sum(pre * sigma * grad, axis=1, keepdims=True)

        total = lax.fori_loop(0, WIDTH // 256, hidden, jnp.zeros((CHUNK_ROWS, 1), F32))
        spread = jnp.where(lane128 == slot128, total, 0.0)
        r.hsend[peers] = jnp.sum(spread.reshape(PER_CHUNK, CAP, 128), axis=1, keepdims=True)

        @pl.loop(0, 2)
        def _(t):
            lo, hi = span(t, 256), span(t + 2, 256)
            first = dot(r.gp_all[rows], r.w_in[lo, :], 1, 1).reshape(PER_CHUNK, CAP, 256)
            last = dot(r.gp_all[rows], r.w_in[hi, :], 1, 1).reshape(PER_CHUNK, CAP, 256)
            r.bsend[peers, :, lo] = jnp.concatenate([first, last], axis=1).astype(BF)

        @pl.when(ch == 0)
        def _():
            r.brecv[0] = r.bsend[0]
            r.hrecv[0] = r.hsend[0]
            for j in range(1, EXP):
                give_back(j, 0, j)

        @pl.when(ch > 0)
        def _():
            for i in range(EXP):
                give_back(base + i, *hop(base + i))

        @pl.loop(EXP, PER_CHUNK)
        def _(i):
            give_back(base + i, *hop(base + i))

    for o in ORDER:
        make_part(1, o, r.u_t, r.gp_all[:, span(lax.rem(me_d + o, DP), PART)])
        reduce_direct(1, o)
    reduce_end(0)

    kv_copies[0].wait_recv()
    kv_copies[1].wait_recv()
    seg_past = r.seg_prev[...] == row8
    augment(past, features(seg_past, listed(group_of), -FAR, 0.0))

    def softmax(b, carry):
        rows = span(b, QROWS)
        window = pl.ds(pl.multiple_of(b * QROWS, QROWS), WINDOW)
        for h in range(4):
            score = dot(r.q_aug[h, rows], r.k_aug[h, window], 1, 1)
            weight = jnp.exp(score - jnp.max(score, axis=1, keepdims=True))
            r.probs[h, rows] = (
                weight * (1.0 / jnp.sum(weight, axis=1, keepdims=True))
            ).astype(BF)
        return carry

    lax.fori_loop(0, BLOCKS // 2, softmax, 0)
    reduce_relay(1, 1)
    reduce_relay(1, 3)
    lax.fori_loop(BLOCKS // 2, BLOCKS, softmax, 0)
    gather_on(0)

    wait_bytes(r.brecv.at[others], r.b_recv)
    back = r.brecv[...].reshape(PEERS * BLOCK, WIDTH // 2)
    for half in range(2):
        cols = slice(half * 512, half * 512 + 512)
        r.dres[:, cols] = (
            r.z_own[:, cols].astype(F32)
            + dot(r.pick[half * TOKENS : (half + 1) * TOKENS, :], back, 1, 0)
        ).astype(BF)
    my_rows = span(me_x, TOKENS)
    do_copies = []
    for o in range(1, EXP):
        px = lax.rem(me_x + o, EXP)
        do_copies.append(
            remote(
                r.dres.at[:, span(px, LOCAL)],
                r.do_all.at[my_rows],
                r.do_send.at[o - 1],
                r.do_recv.at[o - 1],
                {"exp": px},
            )
        )
    r.do_all[my_rows] = r.dres[:, span(me_x, LOCAL)]
    wait_bytes(r.hrecv.at[others], r.h_recv)
    sums = jnp.sum(r.hrecv[...], axis=1)
    lane_s = iota((TOKENS, 128), 1)
    for t in range(2):
        chosen = dot(named[t], sums, 1, 0, lax.Precision.HIGHEST)
        value = jnp.sum(jnp.where(lane_s == slot[t], chosen, 0.0), axis=1, keepdims=True)
        r.dgate[t : t + 1, :] = as_row(value / gates[t]).astype(BF)
    reduce_end(1)
    kv_copies[2].wait_recv()
    for c in do_copies:
        c.wait_recv()

    def backward(b, carry):
        rows = span(b, QROWS)
        window = pl.ds(pl.multiple_of(b * QROWS, QROWS), WINDOW)
        for hp in range(2):
            tile = slice(hp * 128, hp * 128 + 128)
            do_t = r.do_all[rows, tile]
            v_t = r.v_all[window, tile]
            k_t = r.k_all[window, tile]
            all_p, all_s, all_d, all_q, dq = [], [], [], [], []
            for e in range(2):
                keep = low_q if e == 0 else jnp.logical_not(low_q)
                do_e = jnp.where(keep, do_t, none)
                probs = r.probs[2 * hp + e, rows]
                weight = probs.astype(F32)
                grad = dot(do_e, v_t, 1, 1)
                delta = jnp.sum(weight * grad, axis=1, keepdims=True)
                dscore = (weight * (grad - delta)).astype(BF)
                dq.append(dot(dscore, k_t, 1, 0))
                all_p.append(probs)
                all_s.append(dscore)
                all_d.append(do_e)
                all_q.append(jnp.where(keep, r.q_aug[2 * hp + e, rows], none))
            r.dq[rows, tile] = (jnp.where(low_q, dq[0], dq[1]) * 0.125).astype(BF)
            r.acc_k[window, tile] += dot(
                jnp.concatenate(all_s, axis=0), jnp.concatenate(all_q, axis=0), 0, 0
            )
            r.acc_v[window, tile] += dot(
                jnp.concatenate(all_p, axis=0), jnp.concatenate(all_d, axis=0), 0, 0
            )
        return carry

    lax.fori_loop(0, BLOCKS, backward, 0)
    r.over[0] = r.acc_k[:FRAMES].astype(BF)
    r.over[1] = r.acc_v[:FRAMES].astype(BF)
    returned = [
        remote(r.over.at[i], r.came.at[i], r.ret_send.at[i], r.ret_recv.at[i], {"ctx": prior})
        for i in range(2)
    ]
    gather_on(1)
    returned[0].wait_recv()
    r.dk[...] = (r.acc_k[FRAMES:] + r.came[0].astype(F32)).astype(BF)
    returned[1].wait_recv()
    r.dv[...] = (r.acc_v[FRAMES:] + r.came[1].astype(F32)).astype(BF)
    for c in own:
        c.wait()
    for a in range(2):
        for n in (2, 3, 4, 5):
            gathers[a][n].wait_recv()
        for n in range(6):
            gathers[a][n].wait_send()
            reduces[a][n].wait_send()
    for c in do_copies + kv_copies + returned:
        c.wait_send()
    wait_bytes(r.send_u.at[others], r.u_send)
    for n in range(DP):
        wait_bytes(r.send_s.at[n, others], r.s_send.at[n])
    wait_bytes(r.bsend.at[others], r.b_send)
    wait_bytes(r.hsend.at[others], r.h_send)


PIECES = [(name, rows) for name in ("gout", "gin") for rows in range(0, WIDTH, 256)] + [
    (name, None) for name in ("dres", "dq", "dk", "dv", "dgate")
]


def deliver_kernel(*refs):
    n = len(OUTPUTS)
    sources, targets = dict(zip(OUTPUTS, refs)), dict(zip(OUTPUTS, refs[n:]))
    buffers = dict(zip(OUTPUTS, refs[2 * n :]))
    get_sem, put_sem = refs[3 * n :]

    def view(ref, rows):
        return ref if rows is None else ref.at[pl.ds(rows, 256)]

    gets, puts = [], []
    for i, (name, rows) in enumerate(PIECES):
        source, buffer, target = (
            view(group[name], rows) for group in (sources, buffers, targets)
        )
        gets.append(pltpu.make_async_copy(source, buffer, get_sem.at[i]))
        puts.append(pltpu.make_async_copy(buffer, target, put_sem.at[i]))
    for get in gets:
        get.start()
    for get, put in zip(gets, puts):
        get.wait()
        put.start()
    for put in puts:
        put.wait()


def layer(*args):
    vmem = pl.BlockSpec(memory_space=pltpu.VMEM)
    anywhere = pl.BlockSpec(memory_space=pl.ANY)
    frames = jax.ShapeDtypeStruct((FRAMES, LOCAL), BF)
    weight = jax.ShapeDtypeStruct((WIDTH, WIDTH), BF)
    shapes = (
        frames,
        frames,
        frames,
        jax.ShapeDtypeStruct((TOKENS, WIDTH), BF),
        jax.ShapeDtypeStruct((2, TOKENS), BF),
        weight,
        weight,
    )
    results = pl.pallas_call(
        layer_kernel,
        out_shape=shapes,
        in_specs=[anywhere] * len(INPUTS),
        out_specs=(vmem,) * 5 + (anywhere,) * 2,
        scratch_shapes=list(SCRATCH.values()),
        compiler_params=pltpu.CompilerParams(
            collective_id=0, has_side_effects=True, vmem_limit_bytes=VMEM_BYTES
        ),
        name="layer",
    )(*args)
    return pl.pallas_call(
        deliver_kernel,
        out_shape=shapes,
        in_specs=[anywhere] * len(OUTPUTS),
        out_specs=(anywhere,) * len(OUTPUTS),
        scratch_shapes=[pltpu.VMEM(s.shape, s.dtype) for s in shapes]
        + [DMA((len(PIECES),)), DMA((len(PIECES),))],
        compiler_params=pltpu.CompilerParams(vmem_limit_bytes=VMEM_BYTES),
        name="deliver",
    )(*results)


def local(
    queries,
    key_rows,
    value_rows,
    segments,
    left_blocks,
    moe_input,
    out_grad,
    expert_ids,
    gate_weights,
    expert_in,
    expert_out,
):
    dq, dk, dv, d_residual, d_gates, grad_out, grad_in = layer(
        queries[0],
        key_rows[0],
        value_rows[0],
        segments,
        jnp.transpose(left_blocks, (2, 0, 1)),
        moe_input[0],
        out_grad[0],
        expert_ids[0].T,
        gate_weights[0].T,
        expert_in[0],
        expert_out[0],
    )
    return (
        dq[None],
        dk[None],
        dv[None],
        d_residual[None],
        d_gates.T[None],
        grad_in[None],
        grad_out[None],
    )


def solution(mesh):
    assert dict(mesh.shape) == {"dp": DP, "ctx": CTX, "exp": EXP}
    return jax.shard_map(
        local,
        mesh=mesh,
        in_specs=(
            P("dp", "ctx", "exp"),
            P("dp", "ctx", "exp"),
            P("dp", "ctx", "exp"),
            P("dp", "ctx"),
            P("dp", "ctx", None),
            P("dp", ("ctx", "exp"), None),
            P("dp", ("ctx", "exp"), None),
            P("dp", ("ctx", "exp"), None),
            P("dp", ("ctx", "exp"), None),
            P(("ctx", "exp"), None, None),
            P(("ctx", "exp"), None, None),
        ),
        out_specs=(
            P("dp", "ctx", "exp"),
            P("dp", "ctx", "exp"),
            P("dp", "ctx", "exp"),
            P("dp", ("ctx", "exp"), None),
            P("dp", ("ctx", "exp"), None),
            P(("ctx", "exp"), None, None),
            P(("ctx", "exp"), None, None),
        ),
        check_vma=False,
    )
```

time: 309 us -> 134 us (0.43); the launches traced: 305 us -> 134 us
  Pallas kernels: 0 us -> 133 us
  local copies, waits for them, and re-layouts: 83.9 us -> 0 us
  starting transfers between devices: 69.2 us -> 0 us
  waiting for transfers between devices: 54.1 us -> 0 us
  blocking collectives: 37.7 us -> 0 us
  matrix products: 31.1 us -> 0 us
  between operations: 15.2 us -> 0.64 us
  other arithmetic: 13.8 us -> 0 us
    pallas_call x0 -> x2, Pallas kernels: none -> 133 us  [the longest x1 128 us: layer(): pl.pallas_call(layer_kernel, out_shape=shapes, in_specs=[anywhere] * len(...]
    all_to_all x5 -> x0, starting transfers between devices: 54.5 us -> none  [the longest x1 21.5 us: local(): lax.all_to_all(gate_grad.reshape(experts, capacity), ('ctx', 'exp'), spli...]
    all_to_all x1 -> x0, blocking collectives: 37.7 us -> none  [local(): lax.all_to_all(rows_in, ('ctx', 'exp'), split_axis=0, concat_axis=0, tile...]
    psum x1 -> x0, waiting for transfers between devices: 32.1 us -> none  [local(): lax.psum(grad_in.astype(jnp.bfloat16), 'dp').astype(jnp.float32)]
    dot_general x14 -> x0, matrix products: 31.1 us -> none  [the longest x1 4.2 us: expert_backward(): lax.dot_general(scaled, weight_out, (((1,), (1,)), ((), ())), preferred_e...]
    gather x10 -> x0, local copies, waits for them, and re-layouts: 27.4 us -> none  [the longest x2 7.4 us: attention_grads(): key_blocks = key_all[local_index].reshape(n_groups, listed * CH, heads, DH)]
    reshape x10 -> x0, local copies, waits for them, and re-layouts: 21.5 us -> none  [the longest x1 4.66 us: attention_grads(): key_terms.reshape(n_groups, listed, CH * local_width)]
    unnamed x70 -> x0, local copies, waits for them, and re-layouts: 16.2 us -> none
  transfers between devices with their start and end apart: 11 -> 0, of which waited for: 7 -> 0; matrix products, arithmetic and copies ran while one was open for 36% -> 0% of each run, Pallas kernels for 0% -> 0%
where the time goes in v2:
time: 134 us
  Pallas kernels  133 us (99%)
    pallas_call x1, Pallas kernels, layer(): pl.pallas_call(layer_kernel, out_shape=shapes, in_specs=[anywhere] * len(...  128 us
    pallas_call x1, Pallas kernels, layer(): pl.pallas_call(deliver_kernel, out_shape=shapes, in_specs=[anywhere] * le...  4.66 us

profile of v2, /device:TPU:1, one launch (start us, length us, event | category | flops | bytes accessed | tf_op | source)
XLA Modules:
  0.0 133.5 jit_solution(915944040398622094)
XLA Ops:
  0.6 128.2 %layer.1 = (bf16[512,256]{1,0:T(8,128)(2,1)}, bf16[512,256]{1,0:T(8,128)(2,1)}, bf16[512,256]{1,0:T(8,128)(2,1)}, bf16[128,1024]{1,0:T(8,128)(2,1)}, bf16[2,128]...) custom-call(bf16[512,256]{1,0:T(8,128)(2,1)} %bitcast.25, bf16[512,256]{1,0:T(8,128)(2,1)} %bitcast.26, ...), custom_call_target="tpu_custom_call" | custom-call | tf_op jit(solution)/shard_map/layer/pallas_call | solution.py:654
  128.9 4.7 %deliver.1 = (bf16[512,256]{1,0:T(8,128)(2,1)}, bf16[512,256]{1,0:T(8,128)(2,1)}, bf16[512,256]{1,0:T(8,128)(2,1)}, bf16[128,1024]{1,0:T(8,128)(2,1)}, bf16[2,12...) custom-call(bf16[512,256]{1,0:T(8,128)(2,1)} %get-tuple-element.21.refs_0_, ...), custom_call_target="tpu_custom_call" | custom-call | tf_op jit(solution)/shard_map/deliver/pallas_call | solution.py:665

commit v3 on v2

v3 whole, which is shorter than its diff:
```python
import types

import jax
import jax.numpy as jnp
from jax import lax
from jax.experimental import pallas as pl
from jax.experimental.pallas import tpu as pltpu
from jax.sharding import PartitionSpec as P

MESH = pl.DeviceIdType.MESH
BF = jnp.bfloat16
F32 = jnp.float32
I32 = jnp.int32

DP, CTX, EXP = 4, 16, 4
PEERS = CTX * EXP
HALF = CTX // 2
CAP = 8
BLOCK = 2 * CAP
TOKENS = 128
WIDTH = 1024
CHUNKS = 4
PER_CHUNK = PEERS // CHUNKS
CHUNK_ROWS = PER_CHUNK * CAP
ROWS = PEERS * CAP
OTHERS = DP - 1
OTHER_ROWS = OTHERS * CHUNK_ROWS
STEPS = PER_CHUNK // EXP
GROUP = 64
GROUPS = 8
FRAMES = 512
LOCAL = 256
QROWS = 128
BLOCKS = FRAMES // QROWS
WINDOW = FRAMES + QROWS
FAR = 32768.0
VMEM_BYTES = 63 * 1024 * 1024


def dot(a, b, ca, cb, precision=None):
    return lax.dot_general(
        a, b, (((ca,), (cb,)), ((), ())), preferred_element_type=F32, precision=precision
    )


def wait_bytes(ref, sem):
    pltpu.make_async_copy(ref, ref, sem).wait()


def span(index, size):
    return pl.ds(pl.multiple_of(index * size, size), size)


def hop(j):
    s = j // EXP
    return HALF + (2 * (s % 2) - 1) * (s // 2), j % EXP


def iota(shape, dim):
    return lax.broadcasted_iota(I32, shape, dim)


def column(row):
    n = row.shape[1]
    same = iota((n, n), 0) == iota((n, n), 1)
    return jnp.sum(jnp.where(same, row, jnp.zeros_like(row)), axis=1, keepdims=True)


def as_row(col):
    n = col.shape[0]
    same = iota((n, n), 0) == iota((n, n), 1)
    return jnp.sum(jnp.where(same, col, jnp.zeros_like(col)), axis=0, keepdims=True)


INPUTS = ("q", "k", "v", "seg", "lists", "x", "z", "ids", "gate", "win", "wout")
OUTPUTS = ("dq", "dk", "dv", "dres", "dgate", "gout", "gin")
DMA = pltpu.SemaphoreType.DMA
LOADS = ("ids", "gate", "x", "z", "win", "wout", "q", "seg", "lists", "k", "v")
SCRATCH = dict(
    q_own=pltpu.VMEM((FRAMES, LOCAL), BF),
    seg_own=pltpu.VMEM((1, FRAMES), I32),
    lists_own=pltpu.VMEM((3, 1, GROUPS), I32),
    x_own=pltpu.VMEM((TOKENS, WIDTH), BF),
    z_own=pltpu.VMEM((TOKENS, WIDTH), BF),
    ids_own=pltpu.VMEM((2, TOKENS), I32),
    gate_own=pltpu.VMEM((2, TOKENS), BF),
    w_in=pltpu.VMEM((WIDTH, WIDTH), BF),
    w_out=pltpu.VMEM((WIDTH, WIDTH), BF),
    pick_t=pltpu.VMEM((PEERS * BLOCK, 2 * TOKENS), BF),
    gated_t=pltpu.VMEM((PEERS * BLOCK, 2 * TOKENS), BF),
    pick=pltpu.VMEM((2 * TOKENS, PEERS * BLOCK), BF),
    xx=pltpu.VMEM((2 * TOKENS, WIDTH // 2), BF),
    zz=pltpu.VMEM((2 * TOKENS, WIDTH // 2), BF),
    send_u=pltpu.VMEM((PEERS, BLOCK, WIDTH // 2), BF),
    recv_u=pltpu.VMEM((PEERS, BLOCK, WIDTH // 2), BF),
    send_s=pltpu.VMEM((PEERS, BLOCK, WIDTH // 2), BF),
    recv_s=pltpu.VMEM((PEERS, BLOCK, WIDTH // 2), BF),
    gath=pltpu.VMEM((2, OTHERS, PEERS, BLOCK, WIDTH // 2), BF),
    more=pltpu.VMEM((OTHER_ROWS, WIDTH), BF),
    more_gp=pltpu.VMEM((OTHER_ROWS, WIDTH), BF),
    more_u_t=pltpu.VMEM((CHUNKS, WIDTH, OTHER_ROWS), BF),
    more_act_t=pltpu.VMEM((CHUNKS, WIDTH, OTHER_ROWS), BF),
    more_pre=pltpu.VMEM((CHUNKS, OTHER_ROWS, WIDTH), BF),
    acc_in=pltpu.VMEM((WIDTH, WIDTH), F32),
    acc_out=pltpu.VMEM((WIDTH, WIDTH), F32),
    u_chunk=pltpu.VMEM((CHUNK_ROWS, WIDTH), BF),
    u_t=pltpu.VMEM((WIDTH, ROWS), BF),
    act_t=pltpu.VMEM((WIDTH, ROWS), BF),
    pre_all=pltpu.VMEM((ROWS, WIDTH), F32),
    s_all=pltpu.VMEM((ROWS, WIDTH), BF),
    gp_all=pltpu.VMEM((ROWS, WIDTH), BF),
    brecv=pltpu.VMEM((PEERS, BLOCK, WIDTH // 2), BF),
    hsend=pltpu.VMEM((PEERS, 1, 128), F32),
    hrecv=pltpu.VMEM((PEERS, 1, 128), F32),
    k_all=pltpu.VMEM((2 * FRAMES, LOCAL), BF),
    v_all=pltpu.VMEM((2 * FRAMES, LOCAL), BF),
    seg_prev=pltpu.VMEM((1, FRAMES), I32),
    do_all=pltpu.VMEM((FRAMES, LOCAL), BF),
    k_aug=pltpu.VMEM((4, 2 * FRAMES, 128), BF),
    q_aug=pltpu.VMEM((4, FRAMES, 128), BF),
    probs=pltpu.VMEM((4, FRAMES, WINDOW), BF),
    acc_k=pltpu.VMEM((2 * FRAMES, LOCAL), F32),
    acc_v=pltpu.VMEM((2 * FRAMES, LOCAL), F32),
    over=pltpu.VMEM((2, FRAMES, LOCAL), BF),
    came=pltpu.VMEM((2, FRAMES, LOCAL), BF),
    load_sem=DMA((len(LOADS),)),
    u_send=DMA,
    u_recv=DMA((CTX,)),
    s_send=DMA,
    s_recv=DMA((CTX,)),
    b_send=DMA,
    b_recv=DMA,
    h_send=DMA,
    h_recv=DMA,
    ag_send=DMA((2, CHUNKS, 4)),
    ag_recv=DMA((2, CHUNKS, 4)),
    kv_send=DMA((3,)),
    kv_recv=DMA((3,)),
    do_send=DMA((EXP - 1,)),
    do_recv=DMA((EXP - 1,)),
    ret_send=DMA((BLOCKS, 2)),
    ret_recv=DMA((BLOCKS, 2)),
)


def layer_kernel(*refs):
    r = types.SimpleNamespace(**dict(zip(INPUTS + OUTPUTS + tuple(SCRATCH), refs)))
    me_d, me_c, me_x = lax.axis_index("dp"), lax.axis_index("ctx"), lax.axis_index("exp")
    right, left = lax.rem(me_d + 1, DP), lax.rem(me_d + DP - 1, DP)
    after, prior = lax.rem(me_c + 1, CTX), lax.rem(me_c + CTX - 1, CTX)

    targets = dict(
        ids=r.ids_own,
        gate=r.gate_own,
        x=r.x_own,
        z=r.z_own,
        win=r.w_in,
        wout=r.w_out,
        q=r.q_own,
        seg=r.seg_own,
        lists=r.lists_own,
        k=r.k_all.at[pl.ds(FRAMES, FRAMES)],
        v=r.v_all.at[pl.ds(FRAMES, FRAMES)],
    )
    loads = {
        name: pltpu.make_async_copy(getattr(r, name), targets[name], r.load_sem.at[i])
        for i, name in enumerate(LOADS)
    }
    def ahead(k, xo):
        return {"ctx": lax.rem(me_c + k, CTX), "exp": lax.rem(me_x + xo, EXP)}

    def behind(k, xo):
        return {"ctx": lax.rem(me_c - k + CTX, CTX), "exp": lax.rem(me_x - xo + EXP, EXP)}

    def remote(src, dst, ssem, rsem, target):
        copy = pltpu.make_async_remote_copy(
            src_ref=src,
            dst_ref=dst,
            send_sem=ssem,
            recv_sem=rsem,
            device_id=target,
            device_id_type=MESH,
        )
        copy.start()
        return copy

    barrier = pltpu.get_barrier_semaphore()
    for name in LOADS[:4]:
        loads[name].start()
    columns_of = [lax.rem(me_c + k, CTX) for k in range(CTX)]
    rows_of = [lax.rem(me_x + xo, EXP) for xo in range(EXP)]
    for other in (left, right):
        pl.semaphore_signal(barrier, inc=1, device_id={"dp": other}, device_id_type=MESH)
    for k in range(CTX):
        for xo in range(EXP):
            if k or xo:
                pl.semaphore_signal(
                    barrier,
                    inc=1,
                    device_id={"ctx": columns_of[k], "exp": rows_of[xo]},
                    device_id_type=MESH,
                )
    for name in LOADS[4:]:
        loads[name].start()

    def relative(ids):
        k = (ids // EXP - me_c + CTX) % CTX
        xo = (ids % EXP - me_x + EXP) % EXP
        s = jnp.where(k == 0, 0, jnp.where(k < HALF, CTX - 2 * k, 2 * k - CTX + 1))
        return s * EXP + xo

    loads["ids"].wait()
    expert = iota((PEERS, TOKENS), 0)
    peer_row = [relative(r.ids_own[t : t + 1, :]) for t in range(2)]
    named_t = [(peer_row[t] == expert).astype(F32) for t in range(2)]
    before = (iota((TOKENS, TOKENS), 0) < iota((TOKENS, TOKENS), 1)).astype(F32).astype(BF)
    earlier = dot((named_t[0] + named_t[1]).astype(BF), before, 1, 0)
    slot_row = [
        jnp.sum(named_t[t] * earlier, axis=0, keepdims=True).astype(I32) for t in range(2)
    ]
    place_row = [peer_row[t] * BLOCK + slot_row[t] for t in range(2)]
    loads["gate"].wait()
    gate_row = [r.gate_own[t : t + 1, :].astype(F32) for t in range(2)]
    loads["x"].wait()
    r.xx[:TOKENS] = r.x_own[:, : WIDTH // 2]
    r.xx[TOKENS:] = r.x_own[:, WIDTH // 2 :]

    @pl.loop(0, CHUNKS)
    def _(t):
        place = iota((256, TOKENS), 0) + t * 256
        for half in range(2):
            hit = [place_row[i] + half * CAP == place for i in range(2)]
            cols = slice(half * TOKENS, half * TOKENS + TOKENS)
            r.pick_t[span(t, 256), cols] = (hit[0] | hit[1]).astype(F32).astype(BF)
            r.gated_t[span(t, 256), cols] = (
                jnp.where(hit[0], gate_row[0], 0.0) + jnp.where(hit[1], gate_row[1], 0.0)
            ).astype(BF)
        rows = dot(r.pick_t[span(t, 256)], r.xx[...], 1, 0)
        r.send_u[pl.ds(t * 16, 16)] = rows.astype(BF).reshape(16, BLOCK, WIDTH // 2)

    pl.semaphore_wait(barrier, PEERS - 1 + 2)

    past = pl.ds(0, FRAMES)
    kv_copies = [
        remote(r.seg, r.seg_prev, r.kv_send.at[0], r.kv_recv.at[0], {"ctx": after}),
        remote(r.k, r.k_all.at[past], r.kv_send.at[1], r.kv_recv.at[1], {"ctx": after}),
        remote(r.v, r.v_all.at[past], r.kv_send.at[2], r.kv_recv.at[2], {"ctx": after}),
    ]

    def send_rows(j, k, xo):
        remote(r.send_u.at[j], r.recv_u.at[j], r.u_send, r.u_recv.at[j // EXP], ahead(k, xo))

    @pl.loop(EXP, PEERS)
    def _(j):
        send_rows(j, *hop(j))

    for j in range(1, EXP):
        send_rows(j, 0, j)
    r.recv_u[0] = r.send_u[0]

    loads["z"].wait()
    r.zz[:TOKENS] = r.z_own[:, : WIDTH // 2]
    r.zz[TOKENS:] = r.z_own[:, WIDTH // 2 :]

    @pl.loop(0, CHUNKS)
    def _(t):
        rows = dot(r.gated_t[span(t, 256)], r.zz[...], 1, 0)
        r.send_s[pl.ds(t * 16, 16)] = rows.astype(BF).reshape(16, BLOCK, WIDTH // 2)

    def send_grads(j, k, xo):
        remote(r.send_s.at[j], r.recv_s.at[j], r.s_send, r.s_recv.at[j // EXP], ahead(k, xo))

    @pl.loop(EXP, PEERS)
    def _(j):
        send_grads(j, *hop(j))

    for j in range(1, EXP):
        send_grads(j, 0, j)
    r.recv_s[0] = r.send_s[0]

    peer = [column(peer_row[t]) for t in range(2)]
    slot = [column(slot_row[t]) for t in range(2)]
    gates = [column(gate_row[t]) for t in range(2)]
    named = [(peer[t] == iota((TOKENS, PEERS), 1)).astype(F32) for t in range(2)]
    lane_q = iota((TOKENS, PEERS * BLOCK), 1)
    for half in range(2):
        hit = [peer[t] * BLOCK + slot[t] + half * CAP == lane_q for t in range(2)]
        r.pick[pl.ds(half * TOKENS, TOKENS)] = (hit[0] | hit[1]).astype(F32).astype(BF)

    for name in ("q", "seg", "lists", "k", "v"):
        loads[name].wait()
    kinds = 2 * GROUPS
    lane_f, row_f = iota((kinds, 128), 1), iota((kinds, 128), 0)
    place = ((lane_f == row_f) | (lane_f == row_f + 64)).astype(F32).astype(BF)
    row8 = iota((8, FRAMES), 0)
    group_of = iota((8, FRAMES), 1) // GROUP
    moved = []
    for j in range(3):
        lists = column(r.lists_own[j])
        moved.append(jnp.where(lists >= 0, lists - (me_c - 1) * GROUPS, -1))

    def listed(groups):
        return (moved[0] == groups) | (moved[1] == groups) | (moved[2] == groups)

    def features(segment, group, miss, match):
        both = jnp.concatenate(
            [jnp.where(segment, match, miss), jnp.where(group, match, miss)], axis=0
        ).astype(BF)
        return dot(both, place, 0, 0).astype(BF)

    low = iota((FRAMES, 128), 1) < 64
    low_q = iota((QROWS, 128), 1) < 64
    none = jnp.zeros((QROWS, 128), BF)

    def augment(part, feat):
        for hp in range(2):
            k_t = r.k_all[part, hp * 128 : hp * 128 + 128]
            r.k_aug[2 * hp, part] = jnp.where(low, k_t, feat)
            r.k_aug[2 * hp + 1, part] = jnp.where(low, feat, k_t)

    seg_own = r.seg_own[...] == row8
    feat_q = features(seg_own, group_of == row8, 0.0, 1.0)
    for hp in range(2):
        q_t = (r.q_own[:, hp * 128 : hp * 128 + 128].astype(F32) * 0.125).astype(BF)
        r.q_aug[2 * hp] = jnp.where(low, q_t, feat_q)
        r.q_aug[2 * hp + 1] = jnp.where(low, feat_q, q_t)
    list_own = listed(group_of + GROUPS) | (group_of == row8)
    augment(pl.ds(FRAMES, FRAMES), features(seg_own, list_own, -FAR, 0.0))
    r.acc_k[...] = jnp.zeros_like(r.acc_k)
    r.acc_v[...] = jnp.zeros_like(r.acc_v)

    ours = (r.recv_u, r.recv_s)

    def gather(a, ch, n):
        chunk = pl.ds(ch * PER_CHUNK, PER_CHUNK)
        near = pl.ds(ch * PER_CHUNK, PER_CHUNK // 2)
        far = pl.ds(ch * PER_CHUNK + PER_CHUNK // 2, PER_CHUNK // 2)
        src, dst, other = (
            (ours[a].at[chunk], r.gath.at[a, 0, chunk], right),
            (ours[a].at[chunk], r.gath.at[a, 1, chunk], left),
            (r.gath.at[a, 0, near], r.gath.at[a, 2, near], right),
            (r.gath.at[a, 1, far], r.gath.at[a, 2, far], left),
        )[n]
        return pltpu.make_async_remote_copy(
            src_ref=src,
            dst_ref=dst,
            send_sem=r.ag_send.at[a, ch, n],
            recv_sem=r.ag_recv.at[a, ch, n],
            device_id={"dp": other},
            device_id_type=MESH,
        )

    def gather_own(a, ch):
        gather(a, ch, 0).start()
        gather(a, ch, 1).start()

    def gather_on(a, ch):
        gather(a, ch, 0).wait_recv()
        gather(a, ch, 2).start()
        gather(a, ch, 1).wait_recv()
        gather(a, ch, 3).start()

    def gather_wait(a, ch):
        gather(a, ch, 2).wait_recv()
        gather(a, ch, 3).wait_recv()

    def wait_chunk(buffer, sems, ch):
        @pl.when(ch == 0)
        def _():
            wait_bytes(buffer.at[pl.ds(1, EXP - 1)], sems.at[0])

        @pl.when(ch > 0)
        def _():
            wait_bytes(buffer.at[pl.ds(ch * PER_CHUNK, EXP)], sems.at[ch * STEPS])

        for i in range(1, STEPS):
            wait_bytes(buffer.at[pl.ds(ch * PER_CHUNK + i * EXP, EXP)], sems.at[ch * STEPS + i])

    def unpack(blocks):
        came = blocks.astype(F32)
        count = came.shape[0] * CAP
        return [
            came[:, half * CAP : half * CAP + CAP].reshape(count, WIDTH // 2) for half in range(2)
        ]

    def half_cols(half):
        return slice(half * 512, half * 512 + 512)

    def chunk_of_others(a, ch):
        blocks = r.gath[a, :, pl.ds(ch * PER_CHUNK, PER_CHUNK)]
        return blocks.reshape(OTHERS * PER_CHUNK, BLOCK, WIDTH // 2)

    def more_rows(ch):
        for half, u in enumerate(unpack(chunk_of_others(0, ch))):
            r.more[:, half_cols(half)] = u.astype(BF)
            r.more_u_t[ch, half_cols(half)] = u.T.astype(BF)

        @pl.loop(0, WIDTH // 256)
        def _(t):
            cols = span(t, 256)
            pre = dot(r.more[...], r.w_in[:, cols], 1, 0)
            r.more_pre[ch, :, cols] = pre.astype(BF)
            r.more_act_t[ch, cols] = (pre * jax.nn.sigmoid(pre)).T.astype(BF)

    def more_grads(ch):
        for half, s in enumerate(unpack(chunk_of_others(1, ch))):
            r.more[:, half_cols(half)] = s.astype(BF)

        @pl.loop(0, WIDTH // 256)
        def _(t):
            cols = span(t, 256)
            grad = dot(r.more[...], r.w_out[cols, :], 1, 1)
            pre = r.more_pre[ch, :, cols].astype(F32)
            sigma = jax.nn.sigmoid(pre)
            r.more_gp[:, cols] = (grad * sigma * (1.0 + pre * (1.0 - sigma))).astype(BF)

        @pl.loop(0, WIDTH // 256)
        def _(t):
            rows = span(t, 256)
            r.acc_in[rows] += dot(r.more_u_t[ch, rows], r.more_gp[...], 1, 0)
            r.acc_out[rows] += dot(r.more_act_t[ch, rows], r.more[...], 1, 0)

    def softmax(b):
        rows = span(b, QROWS)
        window = pl.ds(pl.multiple_of(b * QROWS, QROWS), WINDOW)
        for h in range(4):
            score = dot(r.q_aug[h, rows], r.k_aug[h, window], 1, 1)
            weight = jnp.exp(score - jnp.max(score, axis=1, keepdims=True))
            r.probs[h, rows] = (
                weight * (1.0 / jnp.sum(weight, axis=1, keepdims=True))
            ).astype(BF)

    loads["win"].wait()
    loads["wout"].wait()

    @pl.loop(0, CHUNKS)
    def _(ch):
        wait_chunk(r.recv_u, r.u_recv, ch)
        gather_own(0, ch)
        rows = span(ch, CHUNK_ROWS)
        for half, u in enumerate(unpack(r.recv_u[pl.ds(ch * PER_CHUNK, PER_CHUNK)])):
            r.u_chunk[:, half_cols(half)] = u.astype(BF)
            r.u_t[half_cols(half), rows] = u.T.astype(BF)

        @pl.loop(0, WIDTH // 256)
        def _(t):
            cols = span(t, 256)
            pre = dot(r.u_chunk[...], r.w_in[:, cols], 1, 0)
            r.pre_all[rows, cols] = pre
            r.act_t[cols, rows] = (pre * jax.nn.sigmoid(pre)).T.astype(BF)

        @pl.when(ch >= 2)
        def _():
            gather_on(0, ch - 2)

        @pl.when(ch == 1)
        def _():
            kv_copies[0].wait_recv()
            kv_copies[1].wait_recv()
            seg_past = r.seg_prev[...] == row8
            augment(past, features(seg_past, listed(group_of), -FAR, 0.0))

        @pl.when(ch >= 1)
        def _():
            softmax(ch - 1)

    softmax(BLOCKS - 1)

    others = pl.ds(1, PEERS - 1)
    wait_bytes(r.send_u.at[others], r.u_send)
    bsend = r.send_u
    lane128 = iota((CHUNK_ROWS, 128), 1)
    slot128 = iota((CHUNK_ROWS, 128), 0) % CAP

    def give_back(j, k, xo):
        remote(bsend.at[j], r.brecv.at[j], r.b_send, r.b_recv, behind(k, xo))
        remote(r.hsend.at[j], r.hrecv.at[j], r.h_send, r.h_recv, behind(k, xo))

    @pl.loop(0, CHUNKS)
    def _(ch):
        base = ch * PER_CHUNK
        rows = span(ch, CHUNK_ROWS)
        peers = pl.ds(base, PER_CHUNK)
        wait_chunk(r.recv_s, r.s_recv, ch)
        gather_own(1, ch)
        for half, s in enumerate(unpack(r.recv_s[peers])):
            r.s_all[rows, half_cols(half)] = s.astype(BF)

        def hidden(t, total):
            cols = span(t, 256)
            grad = dot(r.s_all[rows], r.w_out[cols, :], 1, 1)
            pre = r.pre_all[rows, cols]
            sigma = jax.nn.sigmoid(pre)
            r.gp_all[rows, cols] = (grad * sigma * (1.0 + pre * (1.0 - sigma))).astype(BF)
            return total + jnp.sum(pre * sigma * grad, axis=1, keepdims=True)

        total = lax.fori_loop(0, WIDTH // 256, hidden, jnp.zeros((CHUNK_ROWS, 1), F32))
        spread = jnp.where(lane128 == slot128, total, 0.0)
        r.hsend[peers] = jnp.sum(spread.reshape(PER_CHUNK, CAP, 128), axis=1, keepdims=True)

        @pl.loop(0, 2)
        def _(t):
            lo, hi = span(t, 256), span(t + 2, 256)
            first = dot(r.gp_all[rows], r.w_in[lo, :], 1, 1).reshape(PER_CHUNK, CAP, 256)
            last = dot(r.gp_all[rows], r.w_in[hi, :], 1, 1).reshape(PER_CHUNK, CAP, 256)
            bsend[peers, :, lo] = jnp.concatenate([first, last], axis=1).astype(BF)

        @pl.when(ch == 0)
        def _():
            r.brecv[0] = bsend[0]
            r.hrecv[0] = r.hsend[0]
            for j in range(1, EXP):
                give_back(j, 0, j)

        @pl.when(ch > 0)
        def _():
            for i in range(EXP):
                give_back(base + i, *hop(base + i))

        @pl.loop(EXP, PER_CHUNK)
        def _(i):
            give_back(base + i, *hop(base + i))

        @pl.when(ch < 2)
        def _():
            gather_on(0, ch + 2)

        @pl.when(ch >= 2)
        def _():
            gather_on(1, ch - 2)

        gather_wait(0, ch)
        more_rows(ch)

    @pl.loop(0, WIDTH // 256)
    def _(t):
        rows = span(t, 256)
        r.acc_in[rows] = dot(r.u_t[rows], r.gp_all[...], 1, 0)
        r.acc_out[rows] = dot(r.act_t[rows], r.s_all[...], 1, 0)

    def other_grads(ch, carry):
        gather_wait(1, ch)
        more_grads(ch)
        return carry

    gather_on(1, 2)
    lax.fori_loop(0, 2, other_grads, 0)
    gather_on(1, 3)
    lax.fori_loop(2, 3, other_grads, 0)

    wait_bytes(r.brecv.at[others], r.b_recv)
    back = r.brecv[...].reshape(PEERS * BLOCK, WIDTH // 2)
    for half in range(2):
        cols = slice(half * 512, half * 512 + 512)
        r.dres[:, cols] = (
            r.z_own[:, cols].astype(F32)
            + dot(r.pick[half * TOKENS : (half + 1) * TOKENS, :], back, 1, 0)
        ).astype(BF)
    my_rows = span(me_x, TOKENS)
    do_copies = []
    for o in range(1, EXP):
        px = lax.rem(me_x + o, EXP)
        do_copies.append(
            remote(
                r.dres.at[:, span(px, LOCAL)],
                r.do_all.at[my_rows],
                r.do_send.at[o - 1],
                r.do_recv.at[o - 1],
                {"exp": px},
            )
        )
    r.do_all[my_rows] = r.dres[:, span(me_x, LOCAL)]
    wait_bytes(r.hrecv.at[others], r.h_recv)
    sums = jnp.sum(r.hrecv[...], axis=1)
    lane_s = iota((TOKENS, 128), 1)
    for t in range(2):
        chosen = dot(named[t], sums, 1, 0, lax.Precision.HIGHEST)
        value = jnp.sum(jnp.where(lane_s == slot[t], chosen, 0.0), axis=1, keepdims=True)
        r.dgate[t : t + 1, :] = as_row(value / gates[t]).astype(BF)
    kv_copies[2].wait_recv()
    lax.fori_loop(3, 4, other_grads, 0)
    r.gin[...] = r.acc_in[...].astype(BF)
    r.gout[...] = r.acc_out[...].astype(BF)
    for c in do_copies:
        c.wait_recv()

    def backward(b, carry):
        rows = span(b, QROWS)
        window = pl.ds(pl.multiple_of(b * QROWS, QROWS), WINDOW)
        for hp in range(2):
            tile = slice(hp * 128, hp * 128 + 128)
            do_t = r.do_all[rows, tile]
            v_t = r.v_all[window, tile]
            k_t = r.k_all[window, tile]
            all_p, all_s, all_d, all_q, dq = [], [], [], [], []
            for e in range(2):
                keep = low_q if e == 0 else jnp.logical_not(low_q)
                do_e = jnp.where(keep, do_t, none)
                probs = r.probs[2 * hp + e, rows]
                weight = probs.astype(F32)
                grad = dot(do_e, v_t, 1, 1)
                delta = jnp.sum(weight * grad, axis=1, keepdims=True)
                dscore = (weight * (grad - delta)).astype(BF)
                dq.append(dot(dscore, k_t, 1, 0))
                all_p.append(probs)
                all_s.append(dscore)
                all_d.append(do_e)
                all_q.append(jnp.where(keep, r.q_aug[2 * hp + e, rows], none))
            r.dq[rows, tile] = (jnp.where(low_q, dq[0], dq[1]) * 0.125).astype(BF)
            r.acc_k[window, tile] += dot(
                jnp.concatenate(all_s, axis=0), jnp.concatenate(all_q, axis=0), 0, 0
            )
            r.acc_v[window, tile] += dot(
                jnp.concatenate(all_p, axis=0), jnp.concatenate(all_d, axis=0), 0, 0
            )
        r.over[0, rows] = r.acc_k[rows].astype(BF)
        r.over[1, rows] = r.acc_v[rows].astype(BF)
        for i in range(2):
            give_prior(b, i).start()
        return carry

    def give_prior(b, i):
        rows = span(b, QROWS)
        return pltpu.make_async_remote_copy(
            src_ref=r.over.at[i, rows],
            dst_ref=r.came.at[i, rows],
            send_sem=r.ret_send.at[b, i],
            recv_sem=r.ret_recv.at[b, i],
            device_id={"ctx": prior},
            device_id_type=MESH,
        )

    lax.fori_loop(0, BLOCKS, backward, 0)

    @pl.loop(0, BLOCKS)
    def _(b):
        rows = span(b, QROWS)
        late = pl.ds(pl.multiple_of(FRAMES + b * QROWS, QROWS), QROWS)
        for i, (out, acc) in enumerate(((r.dk, r.acc_k), (r.dv, r.acc_v))):
            give_prior(b, i).wait_recv()
            out[rows] = (acc[late] + r.came[i, rows].astype(F32)).astype(BF)
            give_prior(b, i).wait_send()

    for a in range(2):
        for ch in range(CHUNKS):
            for n in range(4):
                gather(a, ch, n).wait_send()
    for c in do_copies + kv_copies:
        c.wait_send()
    wait_bytes(r.send_s.at[others], r.s_send)
    wait_bytes(bsend.at[others], r.b_send)
    wait_bytes(r.hsend.at[others], r.h_send)


PIECES = [(name, rows) for name in ("gout", "gin") for rows in range(0, WIDTH, 256)] + [
    (name, None) for name in ("dres", "dq", "dk", "dv", "dgate")
]


def deliver_kernel(*refs):
    n = len(OUTPUTS)
    sources, targets = dict(zip(OUTPUTS, refs)), dict(zip(OUTPUTS, refs[n:]))
    buffers = dict(zip(OUTPUTS, refs[2 * n :]))
    get_sem, put_sem = refs[3 * n :]

    def view(ref, rows):
        return ref if rows is None else ref.at[pl.ds(rows, 256)]

    gets, puts = [], []
    for i, (name, rows) in enumerate(PIECES):
        source, buffer, target = (
            view(group[name], rows) for group in (sources, buffers, targets)
        )
        gets.append(pltpu.make_async_copy(source, buffer, get_sem.at[i]))
        puts.append(pltpu.make_async_copy(buffer, target, put_sem.at[i]))
    for get in gets:
        get.start()
    for get, put in zip(gets, puts):
        get.wait()
        put.start()
    for put in puts:
        put.wait()


def layer(*args):
    vmem = pl.BlockSpec(memory_space=pltpu.VMEM)
    anywhere = pl.BlockSpec(memory_space=pl.ANY)
    frames = jax.ShapeDtypeStruct((FRAMES, LOCAL), BF)
    weight = jax.ShapeDtypeStruct((WIDTH, WIDTH), BF)
    shapes = (
        frames,
        frames,
        frames,
        jax.ShapeDtypeStruct((TOKENS, WIDTH), BF),
        jax.ShapeDtypeStruct((2, TOKENS), BF),
        weight,
        weight,
    )
    results = pl.pallas_call(
        layer_kernel,
        out_shape=shapes,
        in_specs=[anywhere] * len(INPUTS),
        out_specs=(vmem,) * 7,
        scratch_shapes=list(SCRATCH.values()),
        compiler_params=pltpu.CompilerParams(
            collective_id=0, has_side_effects=True, vmem_limit_bytes=VMEM_BYTES
        ),
        name="layer",
    )(*args)
    return pl.pallas_call(
        deliver_kernel,
        out_shape=shapes,
        in_specs=[anywhere] * len(OUTPUTS),
        out_specs=(anywhere,) * len(OUTPUTS),
        scratch_shapes=[pltpu.VMEM(s.shape, s.dtype) for s in shapes]
        + [DMA((len(PIECES),)), DMA((len(PIECES),))],
        compiler_params=pltpu.CompilerParams(vmem_limit_bytes=VMEM_BYTES),
        name="deliver",
    )(*results)


def local(
    queries,
    key_rows,
    value_rows,
    segments,
    left_blocks,
    moe_input,
    out_grad,
    expert_ids,
    gate_weights,
    expert_in,
    expert_out,
):
    dq, dk, dv, d_residual, d_gates, grad_out, grad_in = layer(
        queries[0],
        key_rows[0],
        value_rows[0],
        segments,
        jnp.transpose(left_blocks, (2, 0, 1)),
        moe_input[0],
        out_grad[0],
        expert_ids[0].T,
        gate_weights[0].T,
        expert_in[0],
        expert_out[0],
    )
    return (
        dq[None],
        dk[None],
        dv[None],
        d_residual[None],
        d_gates.T[None],
        grad_in[None],
        grad_out[None],
    )


def solution(mesh):
    assert dict(mesh.shape) == {"dp": DP, "ctx": CTX, "exp": EXP}
    return jax.shard_map(
        local,
        mesh=mesh,
        in_specs=(
            P("dp", "ctx", "exp"),
            P("dp", "ctx", "exp"),
            P("dp", "ctx", "exp"),
            P("dp", "ctx"),
            P("dp", "ctx", None),
            P("dp", ("ctx", "exp"), None),
            P("dp", ("ctx", "exp"), None),
            P("dp", ("ctx", "exp"), None),
            P("dp", ("ctx", "exp"), None),
            P(("ctx", "exp"), None, None),
            P(("ctx", "exp"), None, None),
        ),
        out_specs=(
            P("dp", "ctx", "exp"),
            P("dp", "ctx", "exp"),
            P("dp", "ctx", "exp"),
            P("dp", ("ctx", "exp"), None),
            P("dp", ("ctx", "exp"), None),
            P(("ctx", "exp"), None, None),
            P(("ctx", "exp"), None, None),
        ),
        check_vma=False,
    )
```

time: 134 us -> 141 us (1.052)
  Pallas kernels: 133 us -> 140 us
    pallas_call x1, Pallas kernels: 128 us -> 135 us  [layer(): pl.pallas_call(layer_kernel, out_shape=shapes, in_specs=[anywhere] * len(...]
where the time goes in v3:
time: 141 us
  Pallas kernels  140 us (99%)
    pallas_call x1, Pallas kernels, layer(): pl.pallas_call(layer_kernel, out_shape=shapes, in_specs=[anywhere] * len(...  135 us
    pallas_call x1, Pallas kernels, layer(): pl.pallas_call(deliver_kernel, out_shape=shapes, in_specs=[anywhere] * le...  4.66 us

profile of v3, /device:TPU:1, one launch (start us, length us, event | category | flops | bytes accessed | tf_op | source)
XLA Modules:
  0.0 140.6 jit_solution(18348227643177888916)
XLA Ops:
  0.6 135.3 %layer.1 = (bf16[512,256]{1,0:T(8,128)(2,1)}, bf16[512,256]{1,0:T(8,128)(2,1)}, bf16[512,256]{1,0:T(8,128)(2,1)}, bf16[128,1024]{1,0:T(8,128)(2,1)}, bf16[2,128]...) custom-call(bf16[512,256]{1,0:T(8,128)(2,1)} %bitcast.25, bf16[512,256]{1,0:T(8,128)(2,1)} %bitcast.26, ...), custom_call_target="tpu_custom_call" | custom-call | tf_op jit(solution)/shard_map/layer/pallas_call | solution.py:699
  135.9 4.7 %deliver.1 = (bf16[512,256]{1,0:T(8,128)(2,1)}, bf16[512,256]{1,0:T(8,128)(2,1)}, bf16[512,256]{1,0:T(8,128)(2,1)}, bf16[128,1024]{1,0:T(8,128)(2,1)}, bf16[2,12...) custom-call(bf16[512,256]{1,0:T(8,128)(2,1)} %get-tuple-element.21.refs_0_, ...), custom_call_target="tpu_custom_call" | custom-call | tf_op jit(solution)/shard_map/deliver/pallas_call | solution.py:710

commit v4 on v3

--- a/solution.py
+++ b/solution.py
@@ -240,13 +240,6 @@
 
     pl.semaphore_wait(barrier, PEERS - 1 + 2)
 
-    past = pl.ds(0, FRAMES)
-    kv_copies = [
-        remote(r.seg, r.seg_prev, r.kv_send.at[0], r.kv_recv.at[0], {"ctx": after}),
-        remote(r.k, r.k_all.at[past], r.kv_send.at[1], r.kv_recv.at[1], {"ctx": after}),
-        remote(r.v, r.v_all.at[past], r.kv_send.at[2], r.kv_recv.at[2], {"ctx": after}),
-    ]
-
     def send_rows(j, k, xo):
         remote(r.send_u.at[j], r.recv_u.at[j], r.u_send, r.u_recv.at[j // EXP], ahead(k, xo))
 
@@ -277,6 +270,15 @@
     for j in range(1, EXP):
         send_grads(j, 0, j)
     r.recv_s[0] = r.send_s[0]
+
+    past = pl.ds(0, FRAMES)
+    for name in ("seg", "k", "v"):
+        loads[name].wait()
+    kv_copies = [
+        remote(r.seg_own, r.seg_prev, r.kv_send.at[0], r.kv_recv.at[0], {"ctx": after}),
+        remote(r.k_all.at[pl.ds(FRAMES, FRAMES)], r.k_all.at[past], r.kv_send.at[1], r.kv_recv.at[1], {"ctx": after}),
+        remote(r.v_all.at[pl.ds(FRAMES, FRAMES)], r.v_all.at[past], r.kv_send.at[2], r.kv_recv.at[2], {"ctx": after}),
+    ]
 
     peer = [column(peer_row[t]) for t in range(2)]
     slot = [column(slot_row[t]) for t in range(2)]
@@ -287,7 +289,7 @@
         hit = [peer[t] * BLOCK + slot[t] + half * CAP == lane_q for t in range(2)]
         r.pick[pl.ds(half * TOKENS, TOKENS)] = (hit[0] | hit[1]).astype(F32).astype(BF)
 
-    for name in ("q", "seg", "lists", "k", "v"):
+    for name in ("q", "lists"):
         loads[name].wait()
     kinds = 2 * GROUPS
     lane_f, row_f = iota((kinds, 128), 1), iota((kinds, 128), 0)
@@ -453,18 +455,6 @@
         def _():
             gather_on(0, ch - 2)
 
-        @pl.when(ch == 1)
-        def _():
-            kv_copies[0].wait_recv()
-            kv_copies[1].wait_recv()
-            seg_past = r.seg_prev[...] == row8
-            augment(past, features(seg_past, listed(group_of), -FAR, 0.0))
-
-        @pl.when(ch >= 1)
-        def _():
-            softmax(ch - 1)
-
-    softmax(BLOCKS - 1)
 
     others = pl.ds(1, PEERS - 1)
     wait_bytes(r.send_u.at[others], r.u_send)
@@ -544,6 +534,15 @@
         return carry
 
     gather_on(1, 2)
+    kv_copies[0].wait_recv()
+    kv_copies[1].wait_recv()
+    seg_past = r.seg_prev[...] == row8
+    augment(past, features(seg_past, listed(group_of), -FAR, 0.0))
+
+    @pl.loop(0, BLOCKS)
+    def _(b):
+        softmax(b)
+
     lax.fori_loop(0, 2, other_grads, 0)
     gather_on(1, 3)
     lax.fori_loop(2, 3, other_grads, 0)

time: 141 us -> 127 us (0.901)
  Pallas kernels: 140 us -> 126 us
    pallas_call x1, Pallas kernels: 135 us -> 122 us  [layer(): pl.pallas_call(layer_kernel, out_shape=shapes, in_specs=[anywhere] * len(...]
where the time goes in v4:
time: 127 us
  Pallas kernels  126 us (99%)
    pallas_call x1, Pallas kernels, layer(): pl.pallas_call(layer_kernel, out_shape=shapes, in_specs=[anywhere] * len(...  122 us
    pallas_call x1, Pallas kernels, layer(): pl.pallas_call(deliver_kernel, out_shape=shapes, in_specs=[anywhere] * le...  4.66 us

profile of v4, /device:TPU:1, one launch (start us, length us, event | category | flops | bytes accessed | tf_op | source)
XLA Modules:
  0.0 126.9 jit_solution(2835937226223309849)
XLA Ops:
  0.6 121.6 %layer.1 = (bf16[512,256]{1,0:T(8,128)(2,1)}, bf16[512,256]{1,0:T(8,128)(2,1)}, bf16[512,256]{1,0:T(8,128)(2,1)}, bf16[128,1024]{1,0:T(8,128)(2,1)}, bf16[2,128]...) custom-call(bf16[512,256]{1,0:T(8,128)(2,1)} %bitcast.25, bf16[512,256]{1,0:T(8,128)(2,1)} %bitcast.26, ...), custom_call_target="tpu_custom_call" | custom-call | tf_op jit(solution)/shard_map/layer/pallas_call | solution.py:698
  122.3 4.7 %deliver.1 = (bf16[512,256]{1,0:T(8,128)(2,1)}, bf16[512,256]{1,0:T(8,128)(2,1)}, bf16[512,256]{1,0:T(8,128)(2,1)}, bf16[128,1024]{1,0:T(8,128)(2,1)}, bf16[2,12...) custom-call(bf16[512,256]{1,0:T(8,128)(2,1)} %get-tuple-element.21.refs_0_, ...), custom_call_target="tpu_custom_call" | custom-call | tf_op jit(solution)/shard_map/deliver/pallas_call | solution.py:709

commit v5 on v4

--- a/solution.py
+++ b/solution.py
@@ -26,6 +26,7 @@
 OTHERS = DP - 1
 OTHER_ROWS = OTHERS * CHUNK_ROWS
 STEPS = PER_CHUNK // EXP
+EARLY, MIDDLE = 2, 3
 GROUP = 64
 GROUPS = 8
 FRAMES = 512
@@ -451,11 +452,6 @@
             r.pre_all[rows, cols] = pre
             r.act_t[cols, rows] = (pre * jax.nn.sigmoid(pre)).T.astype(BF)
 
-        @pl.when(ch >= 2)
-        def _():
-            gather_on(0, ch - 2)
-
-
     others = pl.ds(1, PEERS - 1)
     wait_bytes(r.send_u.at[others], r.u_send)
     bsend = r.send_u
@@ -511,16 +507,9 @@
         def _(i):
             give_back(base + i, *hop(base + i))
 
-        @pl.when(ch < 2)
+        @pl.when(ch > 0)
         def _():
-            gather_on(0, ch + 2)
-
-        @pl.when(ch >= 2)
-        def _():
-            gather_on(1, ch - 2)
-
-        gather_wait(0, ch)
-        more_rows(ch)
+            gather_on(0, ch - 1)
 
     @pl.loop(0, WIDTH // 256)
     def _(t):
@@ -533,7 +522,6 @@
         more_grads(ch)
         return carry
 
-    gather_on(1, 2)
     kv_copies[0].wait_recv()
     kv_copies[1].wait_recv()
     seg_past = r.seg_prev[...] == row8
@@ -543,9 +531,15 @@
     def _(b):
         softmax(b)
 
-    lax.fori_loop(0, 2, other_grads, 0)
-    gather_on(1, 3)
-    lax.fori_loop(2, 3, other_grads, 0)
+    gather_on(0, CHUNKS - 1)
+
+    @pl.loop(0, CHUNKS)
+    def _(ch):
+        gather_wait(0, ch)
+        more_rows(ch)
+        gather_on(1, ch)
+
+    lax.fori_loop(0, EARLY, other_grads, 0)
 
     wait_bytes(r.brecv.at[others], r.b_recv)
     back = r.brecv[...].reshape(PEERS * BLOCK, WIDTH // 2)
@@ -577,9 +571,7 @@
         value = jnp.sum(jnp.where(lane_s == slot[t], chosen, 0.0), axis=1, keepdims=True)
         r.dgate[t : t + 1, :] = as_row(value / gates[t]).astype(BF)
     kv_copies[2].wait_recv()
-    lax.fori_loop(3, 4, other_grads, 0)
-    r.gin[...] = r.acc_in[...].astype(BF)
-    r.gout[...] = r.acc_out[...].astype(BF)
+    lax.fori_loop(EARLY, MIDDLE, other_grads, 0)
     for c in do_copies:
         c.wait_recv()
 
@@ -630,6 +622,9 @@
         )
 
     lax.fori_loop(0, BLOCKS, backward, 0)
+    lax.fori_loop(MIDDLE, CHUNKS, other_grads, 0)
+    r.gin[...] = r.acc_in[...].astype(BF)
+    r.gout[...] = r.acc_out[...].astype(BF)
 
     @pl.loop(0, BLOCKS)
     def _(b):

time: 127 us -> 124 us (0.976)
  Pallas kernels: 126 us -> 124 us
    pallas_call x1, Pallas kernels: 122 us -> 119 us  [layer(): pl.pallas_call(layer_kernel, out_shape=shapes, in_specs=[anywhere] * len(...]
where the time goes in v5:
time: 124 us
  Pallas kernels  124 us (100%)
    pallas_call x1, Pallas kernels, layer(): pl.pallas_call(layer_kernel, out_shape=shapes, in_specs=[anywhere] * len(...  119 us
    pallas_call x1, Pallas kernels, layer(): pl.pallas_call(deliver_kernel, out_shape=shapes, in_specs=[anywhere] * le...  4.66 us

profile of v5, /device:TPU:1, one launch (start us, length us, event | category | flops | bytes accessed | tf_op | source)
XLA Modules:
  0.0 124.1 jit_solution(6195501156757542989)
XLA Ops:
  0.6 118.8 %layer.1 = (bf16[512,256]{1,0:T(8,128)(2,1)}, bf16[512,256]{1,0:T(8,128)(2,1)}, bf16[512,256]{1,0:T(8,128)(2,1)}, bf16[128,1024]{1,0:T(8,128)(2,1)}, bf16[2,128]...) custom-call(bf16[512,256]{1,0:T(8,128)(2,1)} %bitcast.25, bf16[512,256]{1,0:T(8,128)(2,1)} %bitcast.26, ...), custom_call_target="tpu_custom_call" | custom-call | tf_op jit(solution)/shard_map/layer/pallas_call | solution.py:693
  119.5 4.7 %deliver.1 = (bf16[512,256]{1,0:T(8,128)(2,1)}, bf16[512,256]{1,0:T(8,128)(2,1)}, bf16[512,256]{1,0:T(8,128)(2,1)}, bf16[128,1024]{1,0:T(8,128)(2,1)}, bf16[2,12...) custom-call(bf16[512,256]{1,0:T(8,128)(2,1)} %get-tuple-element.21.refs_0_, ...), custom_call_target="tpu_custom_call" | custom-call | tf_op jit(solution)/shard_map/deliver/pallas_call | solution.py:704

commit v6 on v5

--- a/solution.py
+++ b/solution.py
@@ -535,9 +535,9 @@
 
     @pl.loop(0, CHUNKS)
     def _(ch):
+        gather_on(1, ch)
         gather_wait(0, ch)
         more_rows(ch)
-        gather_on(1, ch)
 
     lax.fori_loop(0, EARLY, other_grads, 0)
 

time: 124 us -> 124 us (level)
  no operation moved by 1% of the time
where the time goes in v6:
time: 124 us
  Pallas kernels  124 us (100%)
    pallas_call x1, Pallas kernels, layer(): pl.pallas_call(layer_kernel, out_shape=shapes, in_specs=[anywhere] * len(...  119 us
    pallas_call x1, Pallas kernels, layer(): pl.pallas_call(deliver_kernel, out_shape=shapes, in_specs=[anywhere] * le...  4.66 us

profile of v6, /device:TPU:1, one launch (start us, length us, event | category | flops | bytes accessed | tf_op | source)
XLA Modules:
  0.0 124.1 jit_solution(17800128841000907691)
XLA Ops:
  0.6 118.8 %layer.1 = (bf16[512,256]{1,0:T(8,128)(2,1)}, bf16[512,256]{1,0:T(8,128)(2,1)}, bf16[512,256]{1,0:T(8,128)(2,1)}, bf16[128,1024]{1,0:T(8,128)(2,1)}, bf16[2,128]...) custom-call(bf16[512,256]{1,0:T(8,128)(2,1)} %bitcast.25, bf16[512,256]{1,0:T(8,128)(2,1)} %bitcast.26, ...), custom_call_target="tpu_custom_call" | custom-call | tf_op jit(solution)/shard_map/layer/pallas_call | solution.py:693
  119.5 4.7 %deliver.1 = (bf16[512,256]{1,0:T(8,128)(2,1)}, bf16[512,256]{1,0:T(8,128)(2,1)}, bf16[512,256]{1,0:T(8,128)(2,1)}, bf16[128,1024]{1,0:T(8,128)(2,1)}, bf16[2,12...) custom-call(bf16[512,256]{1,0:T(8,128)(2,1)} %get-tuple-element.21.refs_0_, ...), custom_call_target="tpu_custom_call" | custom-call | tf_op jit(solution)/shard_map/deliver/pallas_call | solution.py:704
